TPU v7x, 128 devices: a whole 4x4x4 slice. The times are simulated.
128 devices in a mesh: section: 2 (over x_lo), fsdp: 64 (over z, y, x_hi, core).
Axes of the slice: x: 4 (x_hi: 2, x_lo: 2; x = x_hi * 2 + x_lo), y: 4, z: 4, core: 2. Of those that a mesh axis runs over, the one named last changes fastest.
Arguments:
- section_feeds: bfloat16 [2, 2, 4096, 16384], P('section', None, 'fsdp'), may hold values from -6 to 6
- adapter_weights: bfloat16 [2, 16384, 384], P('section', 'fsdp'), as said below
Outputs:
- results: bfloat16 [2, 2, 4096, 16384], P('section', None, 'fsdp')
- weight_grads: bfloat16 [2, 16384, 384], P('section', 'fsdp')
Inputs may be any that keep to these rules, and one draw needn't show every extreme that they name: `adapter_weights`: entries of the down projection have spread about 16384^-0.5 and those of the transposed up projection about 192^-0.5.
All inputs are finite; a program needn't handle non-finite values.
Results may differ from a plain program's by a relative error of at most 0.0075.
Values may be sent and summed in bfloat16 or wider, within the bound.
A program may use at most 128 MiB of HBM per device.

v0:
```python
import jax
import jax.numpy as jnp
from jax import lax
from jax.sharding import PartitionSpec as P

EPSILON = 1e-05


def from_behind(value, axis, steps):
    count = lax.axis_size(axis)
    first, last = (max(0, -steps), min(count, count - steps))
    return lax.ppermute(value, axis, [(source, source + steps) for source in range(first, last)])


def forward(inputs, weight_full):
    low_rank = weight_full.shape[1] // 2
    wide_in = inputs.astype(jnp.float32)
    inverse_rms = lax.rsqrt(jnp.mean(wide_in * wide_in, axis=-1, keepdims=True) + EPSILON)
    normed = (wide_in * inverse_rms).astype(jnp.bfloat16)
    pre_act = jnp.dot(normed, weight_full[:, :low_rank], preferred_element_type=jnp.float32)
    activated = jax.nn.silu(pre_act).astype(jnp.bfloat16)
    branch = lax.dot_general(
        activated,
        weight_full[:, low_rank:],
        (((1,), (1,)), ((), ())),
        preferred_element_type=jnp.float32,
    )
    return ((wide_in + branch).astype(jnp.bfloat16), normed, pre_act, activated, inverse_rms)


def backward(inputs, upstream, weight_full, pre_act, inverse_rms):
    low_rank = weight_full.shape[1] // 2
    act_grad = jnp.dot(upstream, weight_full[:, low_rank:], preferred_element_type=jnp.float32)
    sigmoid_z = jax.nn.sigmoid(pre_act)
    pre_grad = (act_grad * sigmoid_z * (1.0 + pre_act * (1.0 - sigmoid_z))).astype(jnp.bfloat16)
    norm_grad = lax.dot_general(
        pre_grad,
        weight_full[:, :low_rank],
        (((1,), (1,)), ((), ())),
        preferred_element_type=jnp.float32,
    )
    wide_in = inputs.astype(jnp.float32)
    cubed = inverse_rms * inverse_rms * inverse_rms
    input_grad = (
        upstream.astype(jnp.float32)
        + inverse_rms * norm_grad
        - wide_in * cubed * jnp.mean(norm_grad * wide_in, axis=-1, keepdims=True)
    )
    return (input_grad.astype(jnp.bfloat16), pre_grad)


def per_device(section_feeds, adapter_weights):
    first_section = lax.axis_index("section") == 0
    own_shard = adapter_weights[0]
    weight_full = lax.all_gather(own_shard, "fsdp", axis=0, tiled=True)
    low_rank = own_shard.shape[1] // 2
    own_feeds = section_feeds[0]
    micro_count, tokens_dev, model_width = own_feeds.shape
    feed_rows = own_feeds.reshape(micro_count * tokens_dev, model_width)
    rows_count = feed_rows.shape[0]
    zero_wide = jnp.zeros_like(feed_rows)
    zero_narrow = jnp.zeros((rows_count, low_rank), jnp.bfloat16)
    zero_pre = jnp.zeros((rows_count, low_rank), jnp.float32)
    zero_scale = jnp.zeros((rows_count, 1), jnp.float32)
    boundary, normed_a, pre_a, active_a, scale_a = lax.cond(
        first_section,
        lambda: forward(feed_rows, weight_full),
        lambda: (zero_wide, zero_wide, zero_pre, zero_narrow, zero_scale),
    )
    arrived = from_behind(boundary, "section", 1)

    def later_section():
        final_out, normed_b, pre_b, active_b, scale_b = forward(arrived, weight_full)
        passed, grad_b = backward(arrived, feed_rows, weight_full, pre_b, scale_b)
        return (final_out, passed, normed_b, grad_b, active_b)

    final_out, passed, normed_b, grad_b, active_b = lax.cond(
        first_section,
        lambda: (zero_wide, zero_wide, zero_wide, zero_narrow, zero_narrow),
        later_section,
    )
    returned = from_behind(passed, "section", -1)

    def earlier_section():
        return backward(feed_rows, returned, weight_full, pre_a, scale_a)

    input_grad, grad_a = lax.cond(first_section, earlier_section, lambda: (zero_wide, zero_narrow))
    joined = (
        jnp.where(first_section, input_grad, final_out),
        jnp.where(first_section, normed_a, normed_b),
        jnp.where(first_section, grad_a, grad_b),
        jnp.where(first_section, returned, feed_rows),
        jnp.where(first_section, active_a, active_b),
    )
    combined, normed, pre_grad, upstream, activated = joined
    down_part = lax.dot_general(
        normed, pre_grad, (((0,), (0,)), ((), ())), preferred_element_type=jnp.float32
    )
    up_part = lax.dot_general(
        upstream, activated, (((0,), (0,)), ((), ())), preferred_element_type=jnp.float32
    )
    summed = lax.psum_scatter(
        jnp.concatenate([down_part, up_part], axis=1), "fsdp", scatter_dimension=0, tiled=True
    )
    results = combined.reshape(1, micro_count, tokens_dev, model_width)
    return (results, summed.astype(jnp.bfloat16)[None])


def solution(mesh):
    placed = (P("section", None, "fsdp", None), P("section", "fsdp", None))
    return jax.shard_map(
        per_device,
        mesh=mesh,
        in_specs=placed,
        out_specs=(P("section", None, "fsdp", None), P("section", "fsdp", None)),
        check_vma=False,
    )
```

profile of v0, /device:TPU:2, one launch (start us, length us, event | category | flops | bytes accessed | tf_op | source)
XLA Modules:
  0.0 640.3 jit_solution(8099183326938318625)
XLA Ops:
  7.2 0.0 all-gather.3.cloned.1.call-start
  7.2 0.7 all-gather.3.cloned.1.call-update
  7.9 0.0 reduce-scatter.2.cloned.1.call-start
  8.0 97.7 %all-gather.3.cloned.1.call-done = bf16[1,16384,384]{2,1,0:T(8,128)(2,1)} async-done(((bf16[1,256,384]{2,1,0:T(8,128)(2,1)}), bf16[1,16384,384]{2,1,0:T(8,128)(2,1)}) %all-gather.3.cloned.1.call-update) | async-done | bytes 12582928 | tf_op jit(solution)/shard_map/all_gather | solution.py:55
  105.6 3.5 conditional.3
  105.6 0.6 broadcast_in_dim.22
  106.3 2.4 broadcast_in_dim.18.clone
  108.7 0.4 broadcast_in_dim.18
  109.1 1.3 collective-permute-start
  110.4 112.9 %collective-permute-done = bf16[128,16384]{1,0:T(8,128)(2,1)S(1)} collective-permute-done((bf16[128,16384]{1,0:T(8,128)(2,1)S(1)}, bf16[128,16384]{1,0:T(8,128)(2,1)S(1)}, u32[]{:S(2)}, u32[]{:S(2)}) %collective-permute-start) | collective-permute-done | bytes 4194336 | tf_op jit(solution)/shard_map/ppermute | solution.py:12
  223.3 42.5 %conditional.4 = (bf16[128,16384]{1,0:T(8,128)(2,1)}, bf16[128,16384]{1,0:T(8,128)(2,1)S(1)}, bf16[128,16384]{1,0:T(8,128)(2,1)S(1)}, bf16[128,192]{0,1:T(8,128)(2,1)S(1)}, bf16[128,192]{0,1:T(8,128)(2,1)S(1)}) conditional(s32[]{:T(128)} %convert_element_type.54, (bf16[128,16384]{1,0:T(8,128)(2,1)S(1)}, bf16[16384,384]{1,0:T(8,128)(2,1)}, ...), branch_computations={%region_3.6_spmd, %region_6.7_spmd} | conditional | flops 3263513088 | bytes 113645128 | solution.py:77
  223.5 0.9 fusion.8
  224.4 0.8 fusion.9
  225.2 0.0 copy-start.2
  225.2 6.4 %multiply_convert_fusion.1 = (bf16[128,192]{0,1:T(8,128)(2,1)S(1)}, f32[128,192]{0,1:T(8,128)S(1)}) fusion(bf16[128,16384]{1,0:T(8,128)(2,1)S(1)} %fusion.9, bf16[16384,384]{1,0:T(8,128)(2,1)} %get-tuple-element.23), kind=kOutput, calls=%fused_computation.34 | convolution fusion | flops 805429248 | bytes 12730368 | tf_op jit(solution)/shard_map/cond/branch_0_fun/dot_general | solution.py:20
  231.7 0.0 copy-done.2
  231.7 10.2 %fusion.27 = bf16[128,192]{0,1:T(8,128)(2,1)S(1)} fusion(bf16[128,16384]{1,0:T(8,128)(2,1)S(1)} %copy-done.2, bf16[16384,384]{1,0:T(8,128)(2,1)} %get-tuple-element.23, f32[128,192]{0,1:T(8,128)S(1)} %get-tuple-element.65), kind=kOutput, calls=%fused_computation.33 | convolution fusion | flops 805527552 | bytes 12730368 | tf_op jit(solution)/shard_map/cond/branch_0_fun/dot_general | solution.py:33
  241.9 9.7 %fusion.7 = bf16[128,16384]{1,0:T(8,128)(2,1)} fusion(bf16[128,192]{0,1:T(8,128)(2,1)S(1)} %get-tuple-element.84, bf16[128,16384]{1,0:T(8,128)(2,1)S(1)} %get-tuple-element.22, bf16[16384,384]{1,0:T(8,128)(2,1)} %get-tuple-element.23), kind=kOutput, calls=%fused_computation.13 | convolution fusion | flops 811597824 | bytes 16826368 | tf_op jit(solution)/shard_map/cond/branch_0_fun/dot_general | solution.py:22
  251.6 9.4 %fusion.13 = (f32[128]{0:T(128)S(1)}, f32[128,16384]{1,0:T(8,128)}) fusion(bf16[128,16384]{1,0:T(8,128)(2,1)S(1)} %get-tuple-element.22, bf16[128,192]{0,1:T(8,128)(2,1)S(1)} %fusion.27, bf16[16384,384]{1,0:T(8,128)(2,1)} %get-tuple-element.23), kind=kOutput, calls=%fused_computation.23 | convolution fusion | flops 811597696 | bytes 21021184 | tf_op jit(solution)/shard_map/cond/branch_0_fun/dot_general | solution.py:36
  261.0 4.6 fusion.12
  265.9 0.0 copy-start.4
  265.9 3.2 collective-permute-start.1
  269.1 88.1 %collective-permute-done.1 = bf16[128,16384]{1,0:T(8,128)(2,1)} collective-permute-done((bf16[128,16384]{1,0:T(8,128)(2,1)S(1)}, bf16[128,16384]{1,0:T(8,128)(2,1)}, u32[]{:S(2)}, u32[]{:S(2)}) %collective-permute-start.1) | collective-permute-done | bytes 4194336 | tf_op jit(solution)/shard_map/ppermute | solution.py:12
  357.2 0.0 copy-done.4
  357.2 2.6 conditional.5
  357.2 2.3 broadcast_in_dim.28
  359.8 0.0 copy-start
  359.8 4.1 fusion.50
  364.0 0.0 copy-done
  364.0 1.8 fusion.48
  365.8 8.7 %pad_maximum_fusion = f32[16384,384]{0,1:T(8,128)} fusion(f32[16384,192]{0,1:T(8,128)S(1)} %fusion.48, f32[16384,192]{0,1:T(8,128)S(1)} %fusion.50), kind=kLoop, calls=%fused_computation.55 | loop fusion | flops 6291456 | bytes 50331648 | tf_op jit(solution)/shard_map/concatenate | solution.py:103
  374.5 0.0 reduce-scatter.2.cloned.1.call-update
  374.6 4.6 broadcast_select_fusion
  379.2 251.9 %reduce-scatter.2.cloned.1.call-done = f32[256,384]{0,1:T(8,128)} async-done(((f32[16384,384]{0,1:T(8,128)}), f32[256,384]{0,1:T(8,128)}) %reduce-scatter.2.cloned.1.call-update) | async-done | bytes 393232 | tf_op jit(solution)/shard_map/reduce_scatter | solution.py:102
  631.2 1.0 convert_bitcast_fusion
  632.2 0.8 copy.4
  (5 shorter events, 0.0 us)
Async XLA Ops:
  7.2 98.5 %all-gather.3.cloned.1.call-start = ((), (), s32[]{:S(2)}) async-start(), calls=%async_computation.2 | async-start | bytes 12779520 | tf_op jit(solution)/shard_map/all_gather | solution.py:55
  7.9 623.3 %reduce-scatter.2.cloned.1.call-start = ((), (), s32[]{:S(2)}) async-start(), calls=%async_computation.1 | async-start | bytes 25559040 | tf_op jit(solution)/shard_map/reduce_scatter | solution.py:102
  109.1 114.2 %collective-permute-start = (bf16[128,16384]{1,0:T(8,128)(2,1)S(1)}, bf16[128,16384]{1,0:T(8,128)(2,1)S(1)}, u32[]{:S(2)}, u32[]{:S(2)}) collective-permute-start(bf16[128,16384]{1,0:T(8,128)(2,1)S(1)} %get-tuple-element.44), channel_id=1, source_target_pairs={{0,64},{1,65},{2,66},{3,67},{4,68},{5,69},{6,70},{7,71},{8,72},{9,... | collective-permute-start | bytes 12582920 | tf_op jit(solution)/shard_map/ppermute | solution.py:12
  225.2 6.4 %copy-start.2 = (bf16[128,16384]{1,0:T(8,128)(2,1)S(1)}, bf16[128,16384]{1,0:T(8,128)(2,1)}, u32[]{:S(2)}) copy-start(bf16[128,16384]{1,0:T(8,128)(2,1)} %get-tuple-element.24) | copy-start | bytes 12582916 | tf_op jit(solution)/shard_map/cond
  265.9 91.3 %copy-start.4 = (bf16[128,16384]{1,0:T(8,128)(2,1)}, bf16[128,16384]{1,0:T(8,128)(2,1)S(1)}, u32[]{:S(2)}) copy-start(bf16[128,16384]{1,0:T(8,128)(2,1)S(1)} %get-tuple-element.51) | copy-start | bytes 12582916
  265.9 91.3 %collective-permute-start.1 = (bf16[128,16384]{1,0:T(8,128)(2,1)S(1)}, bf16[128,16384]{1,0:T(8,128)(2,1)}, u32[]{:S(2)}, u32[]{:S(2)}) collective-permute-start(bf16[128,16384]{1,0:T(8,128)(2,1)S(1)} %get-tuple-element.45), channel_id=1, source_target_pairs={{64,0},{65,1},{66,2},{67,3},{68,4},{69,5},{70,6},{71,7},{72,8},{73... | collective-permute-start | bytes 12582920 | tf_op jit(solution)/shard_map/ppermute | solution.py:12
  359.8 4.2 copy-start
Sparse Core Ops, SparseCore 0:
  11.1 94.5 all-gather.2
  374.7 256.4 reduce-scatter.1
where the time goes:
time: 649 us; the launch traced here: 640 us
  waiting for transfers between devices  551 us (85%)
  matrix products  41.7 us (6%)
  other arithmetic  20.7 us (3%)
  between operations  14.6 us (2%)
  local copies, waits for them, and re-layouts  6.63 us (1%)
    reduce_scatter x1, waiting for transfers between devices, per_device(): lax.psum_scatter(jnp.concatenate([down_part, up_part], axis=1), 'fsdp', s...  252 us
    ppermute x2, waiting for transfers between devices, from_behind(): lax.ppermute(value, axis, [(source, source + steps) for source in range(f...  201 us
    all_gather x1, waiting for transfers between devices, per_device(): weight_full = lax.all_gather(own_shard, 'fsdp', axis=0, tiled=True)  97.7 us
  transfers between devices with their start and end apart: 4, of which 4 were waited for; matrix products, arithmetic and copies ran while one was open for 1% of the time, Pallas kernels for 0%

commit v1 on v0

v1 whole, which is shorter than its diff:
```python
import functools

import jax
import jax.numpy as jnp
from jax import lax
from jax.experimental import pallas as pl
from jax.experimental.pallas import tpu as pltpu
from jax.sharding import PartitionSpec as P

MESH = pl.DeviceIdType.MESH
EPSILON = 1e-05
BF = jnp.bfloat16
F32 = jnp.float32
NT = (((1,), (1,)), ((), ()))
NN = (((1,), (0,)), ((), ()))
D = 16384
RANK = 192
ROWS = 128
HALF = D // 2
BLK = 256
UNIT = 2 * BLK
EARLY = 9


def dot(a, b, dims):
    return lax.dot_general(a, b, dims, preferred_element_type=F32)


def dot_wide(a, b, dims):
    high = b.astype(BF)
    low = (b - high.astype(F32)).astype(BF)
    return dot(a, high, dims) + dot(a, low, dims)


def away(i):
    return lax.rem(2 + (i * (i + 1)) // 2, 4)


def kernel(
    feed, wt, res, wg,
    own, oth, w, out, gp, r1, r2, send3, r3,
    part, gram, sq, got_part, got_gram, got_sq, sg, got_sg, lr, bg, lrt,
    own_ss, own_rs, own_ls, ex_ss, ex_rs, pre_ss, pre_rs, pre_ls,
    ag_ss, ag_rs, core_ss, core_rs, sg_ss, sg_rs, lr_ss, lr_rs,
    p1_ss, p1_rs, p2_ss, p2_rs, p3_ss, p3_rs, out_ss, out_rs, out_ls,
):
    s = lax.axis_index("section")
    f = lax.axis_index("fsdp")
    c = lax.rem(f, 2)
    xh = lax.rem(f // 2, 2)
    y = lax.rem(f // 4, 4)
    z = f // 16

    def dev(ss=0, dx=0, dy=0, dz=0, dc=0):
        sx = lax.rem(s + ss, 2)
        at = (lax.rem(z + dz, 4) * 4 + lax.rem(y + dy, 4)) * 2 + lax.rem(xh + dx, 2)
        return (sx, at * 2 + lax.rem(c + dc, 2))

    def remote(src, dst, ssem, rsem, to):
        return pltpu.make_async_remote_copy(
            src_ref=src, dst_ref=dst, send_sem=ssem, recv_sem=rsem,
            device_id=to, device_id_type=MESH)

    peers = [dict(dc=1), dict(ss=1), dict(ss=1, dc=1), dict(dx=1), dict(ss=1, dx=1)]
    peers += [dict(dy=d) for d in (1, 2, 3)] + [dict(dz=d) for d in (1, 2, 3)]
    barrier = pltpu.get_barrier_semaphore()
    for peer in peers:
        pl.semaphore_signal(barrier, inc=1, device_id=dev(**peer), device_id_type=MESH)
    pl.semaphore_wait(barrier, len(peers))

    def lanes(dy, dz, h, width=BLK):
        jj = (lax.rem(z + dz, 4) * 4 + lax.rem(y + dy, 4)) * 2 + h
        return pl.ds(pl.multiple_of(jj * BLK, BLK), width)

    def common_rows(section):
        return pl.ds(pl.multiple_of(section * 2 * RANK, RANK), RANK)

    private_rows = pl.ds(RANK, RANK)
    mine = lanes(0, 0, xh)
    place_c = w.at[common_rows(s), mine]
    place_p = w.at[private_rows, mine]
    pre = [
        remote(wt.at[pl.ds(0, RANK)], place_c, pre_ss.at[0], pre_rs.at[0], dev(ss=1)),
        remote(wt.at[pl.ds(0, RANK)], place_c, pre_ss.at[1], pre_rs.at[1], dev(dx=1)),
        remote(wt.at[pl.ds(RANK, RANK)], place_p, pre_ss.at[2], pre_rs.at[2], dev(dx=1)),
        remote(wt.at[pl.ds(0, RANK)], place_c, pre_ss.at[3], pre_rs.at[3], dev(ss=1, dx=1)),
    ]
    for copy in pre:
        copy.start()
    local_pre = [
        pltpu.make_async_copy(wt.at[pl.ds(0, RANK)], place_c, pre_ls.at[0]),
        pltpu.make_async_copy(wt.at[pl.ds(RANK, RANK)], place_p, pre_ls.at[1]),
    ]
    for copy in local_pre:
        copy.start()

    my_rows = pl.ds(pl.multiple_of(c * ROWS, ROWS), ROWS)
    other_rows = pl.ds(pl.multiple_of((1 - c) * ROWS, ROWS), ROWS)

    def feed_at(jj, core):
        return pl.ds(pl.multiple_of(jj * UNIT + core * BLK, BLK), BLK)

    @pl.loop(0, HALF // BLK)
    def _(jj):
        at = pl.ds(pl.multiple_of(jj * BLK, BLK), BLK)
        remote(feed.at[:, feed_at(jj, 1 - c)], own.at[my_rows, at], own_ss, own_rs, dev(dc=1)).start()
        pltpu.make_async_copy(feed.at[:, feed_at(jj, c)], own.at[my_rows, at], own_ls).start()

    def exchange(i):
        dy, dz = away(i // 4), away(lax.rem(i, 4))
        for h in range(2):
            jj = (lax.rem(z + dz, 4) * 4 + lax.rem(y + dy, 4)) * 2 + h
            at = pl.ds(pl.multiple_of(jj * BLK, BLK), BLK)
            for dc in range(2):
                remote(
                    feed.at[:, feed_at(jj, lax.rem(c + dc, 2))], oth.at[my_rows, at],
                    ex_ss, ex_rs.at[i], dev(ss=1, dc=dc)).start()

    pl.loop(0, EARLY)(exchange)

    halves = (pl.ds(0, 3 * RANK // 2), pl.ds(3 * RANK // 2, 3 * RANK // 2))

    def step(h, oa, ob, along_b):
        pass

    def spot(h, oa, ob, rows=slice(None)):
        at = lanes(oa % 4, ob % 4, h) if h == 0 else lanes(ob % 4, oa % 4, h)
        return w.at[rows, at]

    def near(h, b, d):
        return dev(dy=d % 4) if (h == 0) != b else dev(dz=d % 4)

    started = []

    def go(ref, h, g, k, to):
        copy = remote(ref, ref, ag_ss.at[h, g, k], ag_rs.at[h, g, k], to)
        copy.start()
        started.append(copy)

    def came(ref, h, g, k):
        remote(ref, ref, ag_ss.at[h, g, k], ag_rs.at[h, g, k], dev(dy=1)).wait_recv()

    groups = (0, -1, 1, 2)

    def first_sends(h):
        for k, d in ((0, 1), (1, -1)):
            go(spot(h, 0, 0), h, 0, k, near(h, False, d))
        group_sends(h, 1)

    def group_sends(h, g):
        oa = groups[g - 1]
        for k, d in ((0, 1), (1, -1)):
            go(spot(h, oa, 0), h, g, k, near(h, True, d))

    for copy in local_pre:
        copy.wait()

    def arrived(dxh, section, row, k):
        ref = w.at[row, lanes(0, 0, lax.rem(xh + dxh, 2))]
        remote(ref, ref, pre_ss.at[k], pre_rs.at[k], dev(ss=1)).wait_recv()

    arrived(0, 1 - s, common_rows(1 - s), 0)
    arrived(1, s, common_rows(s), 1)
    arrived(1, s, private_rows, 2)
    arrived(1, 1 - s, common_rows(1 - s), 3)
    for h in range(2):
        first_sends(h)
    for h in range(2):
        came(spot(h, -1, 0), h, 0, 0)
        go(spot(h, -1, 0, halves[0]), h, 0, 2, near(h, False, 1))
        group_sends(h, 2)
        came(spot(h, 1, 0), h, 0, 1)
        go(spot(h, 1, 0, halves[1]), h, 0, 3, near(h, False, -1))
        group_sends(h, 3)

    def forward(h, g):
        oa = groups[g - 1]
        came(spot(h, oa, -1), h, g, 0)
        go(spot(h, oa, -1, halves[0]), h, g, 2, near(h, True, 1))
        came(spot(h, oa, 1), h, g, 1)
        go(spot(h, oa, 1, halves[1]), h, g, 3, near(h, True, -1))

    for h in range(2):
        forward(h, 1)
    for h in range(2):
        came(spot(h, 2, 0, halves[0]), h, 0, 2)
        came(spot(h, 2, 0, halves[1]), h, 0, 3)
        group_sends(h, 4)
    for g in (2, 3, 4):
        for h in range(2):
            forward(h, g)
    for g in (1, 2, 3, 4):
        for h in range(2):
            oa = groups[g - 1]
            came(spot(h, oa, 2, halves[0]), h, g, 2)
            came(spot(h, oa, 2, halves[1]), h, g, 3)

    whole = own.at[my_rows, :]
    pltpu.make_async_copy(whole, whole, own_ls).wait()
    there = own.at[other_rows, :]
    remote(there, there, own_ss, own_rs, dev(dc=1)).wait_recv()
    part[...] = jnp.zeros_like(part)
    gram[...] = jnp.zeros_like(gram)
    sq[...] = jnp.zeros_like(sq)

    @pl.loop(0, HALF // 1024)
    def _(k):
        at = pl.ds(pl.multiple_of(k * 1024, 1024), 1024)
        x = own[:, at]
        for m in range(3):
            part[m] += dot(x, w[pl.ds(m * RANK, RANK), at], NT)
        u = w[pl.ds(0, RANK), at]
        gram[0] += dot(u, u, NT)
        gram[1] += dot(u, w[pl.ds(2 * RANK, RANK), at], NT)
        xf = x.astype(F32)
        sq[...] += jnp.broadcast_to(jnp.sum(xf * xf, axis=1, keepdims=True), sq.shape)

    to_core = [
        remote(part.at[:, other_rows], got_part, core_ss.at[0], core_rs.at[0], dev(dc=1)),
        remote(gram, got_gram, core_ss.at[1], core_rs.at[1], dev(dc=1)),
        remote(sq.at[other_rows], got_sq, core_ss.at[2], core_rs.at[2], dev(dc=1)),
    ]
    for copy in to_core:
        copy.start()
    for copy in to_core:
        copy.wait()
    sums = [part[m, my_rows] + got_part[m] for m in range(3)]
    from_later = remote(sg, got_sg, sg_ss, sg_rs, dev(ss=1))

    lr_mine = lr.at[:, my_rows]
    bg_mine = bg.at[:, my_rows]
    three = lr.at[pl.ds(0, 3), my_rows]
    to_lr = [
        remote(three, three, lr_ss.at[0], lr_rs.at[c], dev(ss=1)),
        remote(three, three, lr_ss.at[1], lr_rs.at[c], dev(ss=1, dc=1)),
        remote(lr_mine, lr_mine, lr_ss.at[2], lr_rs.at[2], dev(dc=1)),
        remote(bg_mine, bg_mine, lr_ss.at[3], lr_rs.at[3], dev(dc=1)),
    ]

    @pl.when(s == 1)
    def _():
        sg[0] = sums[0]
        sg[1] = sums[1]
        from_later.start()
        from_later.wait_send()
        for core in range(2):
            ref = lr.at[pl.ds(0, 3), pl.ds(core * ROWS, ROWS)]
            remote(ref, ref, lr_ss.at[0], lr_rs.at[core], dev(ss=1)).wait_recv()

    @pl.when(s == 0)
    def _():
        from_later.wait_recv()
        q0, p0, r = sums
        g0, g1 = got_sg[0], got_sg[1]
        uu = gram[0] + got_gram[0]
        ua = gram[1] + got_gram[1]
        sx = (sq[my_rows] + got_sq[...])[:, :1]
        inv0 = lax.rsqrt(sx * (1.0 / D) + EPSILON)
        pre0 = p0 * inv0
        sig0 = 1.0 / (1.0 + jnp.exp(-pre0))
        act0 = (pre0 * sig0).astype(BF)
        act0f = act0.astype(F32)
        t = dot_wide(act0, uu, NN)
        sb = sx + jnp.sum(act0f * (2.0 * q0 + t), axis=1, keepdims=True)
        inv1 = lax.rsqrt(jnp.maximum(sb, 0.0) * (1.0 / D) + EPSILON)
        p1 = r + dot_wide(act0, ua, NN)
        pre1 = p1 * inv1
        sig1 = 1.0 / (1.0 + jnp.exp(-pre1))
        act1 = (pre1 * sig1).astype(BF)
        pg1 = (g1 * sig1 * (1.0 + pre1 * (1.0 - sig1))).astype(BF).astype(F32)
        beta = inv1 * inv1 * inv1 * (jnp.sum(pg1 * p1, axis=1, keepdims=True) * (1.0 / D))
        pg1s = (pg1 * inv1).astype(BF)
        ag0 = g0 + dot_wide(pg1s, ua, NT) - beta * (q0 + t)
        pg0 = (ag0 * sig0 * (1.0 + pre0 * (1.0 - sig0))).astype(BF).astype(F32)
        gamma = inv0 * inv0 * inv0 * (jnp.sum(pg0 * p0, axis=1, keepdims=True) * (1.0 / D))
        lr[0, my_rows] = act0
        lr[1, my_rows] = pg1s
        lr[2, my_rows] = act1
        lr[3, my_rows] = (pg0 * inv0).astype(BF)
        bg[0, my_rows] = jnp.broadcast_to(beta, (ROWS, 128))
        bg[1, my_rows] = jnp.broadcast_to(gamma, (ROWS, 128))
        for copy in to_lr:
            copy.start()
        lr_other = lr.at[:, other_rows]
        bg_other = bg.at[:, other_rows]
        remote(lr_other, lr_other, lr_ss.at[2], lr_rs.at[2], dev(dc=1)).wait_recv()
        remote(bg_other, bg_other, lr_ss.at[3], lr_rs.at[3], dev(dc=1)).wait_recv()
        for copy in to_lr:
            copy.wait_send()

    pl.loop(EARLY, 16)(exchange)

    @pl.when(s == 0)
    def _():
        lrt[0] = lr[3].astype(F32).T.astype(BF)
        lrt[1] = lr[0].astype(F32).T.astype(BF)

    @pl.when(s == 1)
    def _():
        lrt[0] = lr[1].astype(F32).T.astype(BF)
        lrt[1] = lr[2].astype(F32).T.astype(BF)

    @pl.loop(0, 16)
    def _(i):
        dy, dz = away(i // 4), away(lax.rem(i, 4))
        jj = (lax.rem(z + dz, 4) * 4 + lax.rem(y + dy, 4)) * 2
        at = pl.ds(pl.multiple_of(jj * BLK, UNIT), UNIT)
        new = oth.at[:, at]
        remote(new, new, ex_ss, ex_rs.at[i], dev(ss=1)).wait_recv()
        u0 = w[pl.ds(0, RANK), at]
        v = w[pl.ds(RANK, RANK), at]
        a1 = w[pl.ds(2 * RANK, RANK), at]

        @pl.when(s == 0)
        def _():
            x, g = own[:, at], oth[:, at]
            xf = x.astype(F32)
            beta = bg[0][:, :1]
            gamma = bg[1][:, :1]
            b = (xf + dot(lr[0], u0, NN)).astype(BF).astype(F32)
            passed = (g.astype(F32) + dot(lr[1], a1, NN) - beta * b).astype(BF)
            out[:, at] = (passed.astype(F32) + dot(lr[3], v, NN) - gamma * xf).astype(BF)
            gp[pl.ds(0, RANK), at] = dot(lrt[0], x, NN).astype(BF)
            gp[pl.ds(RANK, RANK), at] = dot(lrt[1], passed, NN).astype(BF)

        @pl.when(s == 1)
        def _():
            x, g = oth[:, at], own[:, at]
            b = (x.astype(F32) + dot(lr[0], u0, NN)).astype(BF)
            out[:, at] = (b.astype(F32) + dot(lr[2], v, NN)).astype(BF)
            gp[pl.ds(0, RANK), at] = dot(lrt[0], b, NN).astype(BF)
            gp[pl.ds(RANK, RANK), at] = dot(lrt[1], g, NN).astype(BF)

        for h in range(2):
            here = pl.ds(pl.multiple_of((jj + h) * BLK, BLK), BLK)
            there = res.at[:, feed_at(jj + h, c)]
            pltpu.make_async_copy(out.at[my_rows, here], there, out_ls).start()
            remote(out.at[other_rows, here], there, out_ss, out_rs, dev(dc=1)).start()

        @pl.when(dy != 0)
        def _():
            dst = r1.at[0, dy - 1, :, pl.ds(pl.multiple_of(dz * UNIT, UNIT), UNIT)]
            remote(gp.at[pl.ds(0, RANK), at], dst, p1_ss.at[0], p1_rs.at[0, dy - 1, dz], dev(dy=dy)).start()

        @pl.when(dz != 0)
        def _():
            dst = r1.at[1, dz - 1, :, pl.ds(pl.multiple_of(dy * UNIT, UNIT), UNIT)]
            remote(gp.at[pl.ds(RANK, RANK), at], dst, p1_ss.at[1], p1_rs.at[1, dz - 1, dy], dev(dz=dz)).start()

    second = []
    for d in (2, 1, 3, 0):
        for h in (1, 0):
            at = lanes(0, d, 0, UNIT) if h == 0 else lanes(d, 0, 0, UNIT)
            ref = gp.at[pl.ds(h * RANK, RANK), at]
            total = ref[...].astype(F32)
            for k in range(3):
                src = r1.at[h, k, :, pl.ds(d * UNIT, UNIT)]
                remote(src, src, p1_ss.at[h], p1_rs.at[h, k, d], dev(dy=1)).wait_recv()
                total += src[...].astype(F32)
            ref[...] = total.astype(BF)
            if d:
                to = dev(dz=d) if h == 0 else dev(dy=d)
                copy = remote(ref, r2.at[h, d - 1], p2_ss.at[h, d - 1], p2_rs.at[h, d - 1], to)
                copy.start()
                second.append(copy)
    for copy in second:
        copy.wait()
    third = []
    for h in range(2):
        total = gp[pl.ds(h * RANK, RANK), lanes(0, 0, 0, UNIT)].astype(F32)
        for k in range(3):
            total += r2[h, k].astype(F32)
        low = xh == 0
        wg[pl.ds(h * RANK, RANK)] = jnp.where(low, total[:, :BLK], total[:, BLK:])
        send3[h] = jnp.where(low, total[:, BLK:], total[:, :BLK]).astype(BF)
        copy = remote(send3.at[h], r3.at[h], p3_ss.at[h], p3_rs.at[h], dev(dx=1))
        copy.start()
        third.append(copy)
    for h, copy in enumerate(third):
        copy.wait()
        wg[pl.ds(h * RANK, RANK)] += r3[h].astype(F32)

    for copy in pre + started:
        copy.wait_send()
    remote(there_all(own, other_rows), there_all(own, other_rows), own_ss, own_rs, dev(dc=1)).wait_send()
    remote(oth, oth, ex_ss, ex_rs.at[0], dev(ss=1)).wait_send()

    @pl.when(s == 1)
    def _():
        pass

    for h in range(2):
        ref = gp.at[pl.ds(h * RANK, RANK), pl.ds(0, 12 * UNIT)]
        remote(ref, ref, p1_ss.at[h], p1_rs.at[h, 0, 0], dev(dy=1)).wait_send()
    half = out.at[my_rows, :]
    pltpu.make_async_copy(half, half, out_ls).wait()
    remote(half, half, out_ss, out_rs, dev(dc=1)).wait()


def there_all(ref, rows):
    return ref.at[rows, :]


def per_device(section_feeds, adapter_weights):
    shard = adapter_weights[0]
    feed = section_feeds[0].reshape(ROWS, D)
    first = lax.axis_index("section") == 0
    down, up = shard[:, :RANK].T, shard[:, RANK:].T
    wt = jnp.where(first, jnp.concatenate([up, down]), jnp.concatenate([down, up]))
    dma = pltpu.SemaphoreType.DMA
    vm = pltpu.VMEM
    res, wg = pl.pallas_call(
        kernel,
        out_shape=(jax.ShapeDtypeStruct((ROWS, D), BF), jax.ShapeDtypeStruct((2 * RANK, BLK), F32)),
        in_specs=[pl.BlockSpec(memory_space=pl.ANY), pl.BlockSpec(memory_space=pltpu.VMEM)],
        out_specs=(pl.BlockSpec(memory_space=pl.ANY), pl.BlockSpec(memory_space=pltpu.VMEM)),
        scratch_shapes=[
            vm((2 * ROWS, HALF), BF), vm((2 * ROWS, HALF), BF), vm((3 * RANK, HALF), BF),
            vm((2 * ROWS, HALF), BF), vm((2 * RANK, HALF), BF),
            vm((2, 3, RANK, 4 * UNIT), BF), vm((2, 3, RANK, UNIT), BF),
            vm((2, RANK, BLK), BF), vm((2, RANK, BLK), BF),
            vm((3, 2 * ROWS, RANK), F32), vm((2, RANK, RANK), F32), vm((2 * ROWS, 128), F32),
            vm((3, ROWS, RANK), F32), vm((2, RANK, RANK), F32), vm((ROWS, 128), F32),
            vm((2, ROWS, RANK), F32), vm((2, ROWS, RANK), F32),
            vm((4, 2 * ROWS, RANK), BF), vm((2, 2 * ROWS, 128), F32), vm((2, RANK, 2 * ROWS), BF),
            dma, dma, dma, dma, dma((16,)), dma((4,)), dma((4,)), dma((2,)),
            dma((2, 5, 4)), dma((2, 5, 4)), dma((3,)), dma((3,)), dma, dma, dma((4,)), dma((4,)),
            dma((2,)), dma((2, 3, 4)), dma((2, 3)), dma((2, 3)), dma((2,)), dma((2,)), dma, dma, dma,
        ],
        compiler_params=pltpu.CompilerParams(
            collective_id=0, has_side_effects=True, vmem_limit_bytes=60 * 2**20),
        cost_estimate=pl.CostEstimate(flops=8 * 10**9, bytes_accessed=10**7, transcendentals=0),
        name="relay",
    )(feed, wt)
    return res.reshape(section_feeds.shape), wg.T.astype(BF)[None]


def solution(mesh):
    placed = (P("section", None, "fsdp", None), P("section", "fsdp", None))
    return jax.shard_map(per_device, mesh=mesh, in_specs=placed, out_specs=placed, check_vma=False)
```

time: 649 us -> 165 us (0.25)
  the two profiles are of different devices: /device:TPU:2 before, /device:TPU:1 now
where the time goes in v1:
time: 165 us; the launch traced here: 164 us
  Pallas kernels  155 us (94%)
  local copies, waits for them, and re-layouts  6.46 us (4%)
  other arithmetic  1.76 us (1%)
    pallas_call x1, Pallas kernels, per_device(): pl.pallas_call(kernel, out_shape=(jax.ShapeDtypeStruct((ROWS, D), BF), ja...  155 us
    unnamed x3, local copies, waits for them, and re-layouts  6.45 us

profile of v1, /device:TPU:1, one launch (start us, length us, event | category | flops | bytes accessed | tf_op | source)
XLA Modules:
  0.0 164.4 jit_solution(4339970565113752863)
XLA Ops:
  0.6 1.1 copy.4
  1.7 0.7 maximum_select_fusion.wt
  2.5 155.5 %relay.1 = (bf16[128,16384]{1,0:T(8,128)(2,1)}, f32[384,256]{1,0:T(8,128)}) custom-call(bf16[128,16384]{1,0:T(8,128)(2,1)} %bitcast.13, bf16[384,256]{1,0:T(8,128)(2,1)} %maximum_select_fusion.wt), custom_call_target="tpu_custom_call" | custom-call | flops 8000000000 | bytes 10000000 | tf_op jit(solution)/shard_map/relay/pallas_call | solution.py:412
  158.0 1.0 convert_bitcast_fusion
  159.0 0.8 copy.5
  159.8 4.6 %copy.7 = bf16[1,2,64,16384]{3,2,1,0:T(8,128)(2,1)} copy(bf16[1,2,64,16384]{3,2,1,0:T(8,128)(2,1)} %bitcast.11) | data formatting | bytes 8388608
  (1 shorter events, 0.0 us)

commit v2 on v0

v2 whole, which is shorter than its diff:
```python
import jax
import jax.numpy as jnp
from jax import lax
from jax.experimental import pallas as pl
from jax.experimental.pallas import tpu as pltpu
from jax.sharding import PartitionSpec as P

MESH = pl.DeviceIdType.MESH
EPSILON = 1e-05
BF = jnp.bfloat16
F32 = jnp.float32
NT = (((1,), (1,)), ((), ()))
NN = (((1,), (0,)), ((), ()))
D = 16384
RANK = 192
ROWS = 128
HALF = D // 2
BLK = 256
RING = 4 * BLK
PACE = ((2, 4, 5, 6, 7, 9, 10), (2, 3, 4, 5, 6, 6, 6))
FROM_BACK = (2, 3, 1, 0)


def dot(a, b, dims):
    return lax.dot_general(a, b, dims, preferred_element_type=F32)


def dot_wide(a, b, dims):
    high = b.astype(BF)
    low = (b - high.astype(F32)).astype(BF)
    return dot(a, high, dims) + dot(a, low, dims)


def away(i):
    return lax.rem(2 + (i * (i + 1)) // 2, 4)


def kernel(
    feed, wt, res, wg,
    own, oth, w, out, gp, r0, r1, r2, tot, send3, r3,
    part, gram, sq, got_part, got_gram, got_sq, sg, got_sg, lr, bg, lrt,
    own_ss, own_rs, own_ls, ex_ss, ex_rs, pre_ss, pre_rs, pre_ls,
    ag_ss, ag_rs, core_ss, core_rs, sg_ss, sg_rs, lr_ss, lr_rs,
    p0_ss, p0_rs, p1_ss, p1_rs, p2_ss, p2_rs, p3_ss, p3_rs, out_ss, out_rs, out_ls,
):
    s = lax.axis_index("section")
    f = lax.axis_index("fsdp")
    c = lax.rem(f, 2)
    xh = lax.rem(f // 2, 2)
    y = lax.rem(f // 4, 4)
    z = f // 16

    def dev(ss=0, dx=0, dy=0, dz=0, dc=0):
        sx = lax.rem(s + ss, 2)
        at = (lax.rem(z + dz, 4) * 4 + lax.rem(y + dy, 4)) * 2 + lax.rem(xh + dx, 2)
        return (sx, at * 2 + lax.rem(c + dc, 2))

    def remote(src, dst, ssem, rsem, to):
        return pltpu.make_async_remote_copy(
            src_ref=src, dst_ref=dst, send_sem=ssem, recv_sem=rsem,
            device_id=to, device_id_type=MESH)

    other_core, later = dev(dc=1), dev(ss=1)

    def place(r, oa, ob):
        pa, pb = y * (1 - r) + z * r, z * (1 - r) + y * r
        return lax.rem(pa + oa, 4), lax.rem(pb + ob, 4)

    def lanes(r, oa, ob):
        a, b = place(r, oa, ob)
        return pl.ds(pl.multiple_of(((r * 4 + a) * 4 + b) * BLK, BLK), BLK)

    def group_lanes(r, oa):
        a, _ = place(r, oa, 0)
        return pl.ds(pl.multiple_of((r * 4 + a) * RING, RING), RING)

    def feed_at(r, a, b, core):
        jj = (b * (1 - r) + a * r) * 4 + a * (1 - r) + b * r
        return pl.ds(pl.multiple_of(((jj * 2 + lax.rem(xh + r, 2)) * 2 + core) * BLK, BLK), BLK)

    def along(r, d, second):
        if isinstance(r, int):
            return dev(dy=d) if (r == 0) != second else dev(dz=d)
        return dev(dy=d * (1 - r), dz=d * r) if not second else dev(dy=d * r, dz=d * (1 - r))

    peers = [dict(dc=1), dict(ss=1), dict(ss=1, dc=1), dict(dx=1), dict(ss=1, dx=1)]
    peers += [dict(dy=d) for d in (1, 2, 3)] + [dict(dz=d) for d in (1, 2, 3)]
    barrier = pltpu.get_barrier_semaphore()
    for peer in peers:
        pl.semaphore_signal(barrier, inc=1, device_id=dev(**peer), device_id_type=MESH)
    pl.semaphore_wait(barrier, len(peers))

    my_rows = pl.ds(pl.multiple_of(c * ROWS, ROWS), ROWS)
    other_rows = pl.ds(pl.multiple_of((1 - c) * ROWS, ROWS), ROWS)

    def exchange(i):
        for r in range(2):
            oa, ob = away(i // 4), away(lax.rem(i, 4))
            a, b = place(r, oa, ob)
            for dc in range(2):
                remote(
                    feed.at[:, feed_at(r, a, b, lax.rem(c + dc, 2))], oth.at[my_rows, lanes(r, oa, ob)],
                    ex_ss, ex_rs.at[i, r], dev(ss=1, dc=dc)).start()

    def fill():
        @pl.loop(0, 32)
        def _(k):
            r, a, b = k // 16, lax.rem(k // 4, 4), lax.rem(k, 4)
            at = pl.ds(pl.multiple_of(k * BLK, BLK), BLK)
            remote(feed.at[:, feed_at(r, a, b, 1 - c)], own.at[my_rows, at], own_ss, own_rs, other_core).start()
            pltpu.make_async_copy(feed.at[:, feed_at(r, a, b, c)], own.at[my_rows, at], own_ls).start()

    def filled():
        whole = own.at[my_rows, :]
        pltpu.make_async_copy(whole, whole, own_ls).wait()
        there = own.at[other_rows, :]
        remote(there, there, own_ss, own_rs, other_core).wait_recv()

    def gather(section):
        rows = (3 if section == 0 else 2) * RANK
        halves = (pl.ds(0, rows // 2), pl.ds(rows // 2, rows // 2))
        begun = 0
        points = iter(PACE[section])

        def pace():
            nonlocal begun
            upto = next(points)
            if upto > begun:
                pl.loop(begun, upto)(exchange)
            begun = upto

        near, far = lanes(0, 0, 0), lanes(1, 0, 0)
        first, both = pl.ds(0, RANK), pl.ds(0, 2 * RANK)
        middle, last = pl.ds(RANK, RANK), pl.ds(2 * RANK, RANK)
        sent, kept = (first, both) if section == 0 else (last, middle)
        got = last if section == 0 else first
        pre = [
            remote(wt.at[first], w.at[sent, near], pre_ss.at[0], pre_rs.at[0], later),
            remote(wt.at[kept], w.at[kept, far], pre_ss.at[2], pre_rs.at[2], dev(dx=1)),
            remote(wt.at[first], w.at[sent, far], pre_ss.at[1], pre_rs.at[1], dev(ss=1, dx=1)),
        ]
        for copy in pre:
            copy.start()
        local = pltpu.make_async_copy(wt.at[kept], w.at[kept, near], pre_ls)
        local.start()
        pace()

        def arrived(rows, at, k):
            remote(w.at[rows, at], w.at[rows, at], pre_ss.at[k], pre_rs.at[k], later).wait_recv()

        def spot(r, oa, ob, part_rows=pl.ds(0, rows)):
            return w.at[part_rows, lanes(r, oa % 4, ob % 4)]

        started = list(pre)

        def go(ref, r, g, k, to):
            copy = remote(ref, ref, ag_ss.at[r, g, k], ag_rs.at[r, g, k], to)
            copy.start()
            started.append(copy)

        def came(ref, r, g, k):
            remote(ref, ref, ag_ss.at[r, g, k], ag_rs.at[r, g, k], later).wait_recv()

        order = (0, -1, 1, 2)

        def group_sends(r, g):
            for k, d in ((0, 1), (1, 3)):
                go(spot(r, order[g - 1], 0), r, g, k, along(r, d, True))

        def first_sends(r):
            for k, d in ((0, 1), (1, 3)):
                go(spot(r, 0, 0), r, 0, k, along(r, d, False))
            group_sends(r, 1)

        def forward(r, g):
            oa = order[g - 1]
            came(spot(r, oa, -1), r, g, 0)
            go(spot(r, oa, -1, halves[0]), r, g, 2, along(r, 1, True))
            came(spot(r, oa, 1), r, g, 1)
            go(spot(r, oa, 1, halves[1]), r, g, 3, along(r, 3, True))

        def complete(r, g):
            oa = order[g - 1]
            came(spot(r, oa, 2, halves[0]), r, g, 2)
            came(spot(r, oa, 2, halves[1]), r, g, 3)

        def products(g):
            @pl.loop(0, 2)
            def _(r):
                at = group_lanes(r, order[g - 1] % 4)
                x = own[:, at]
                for m in range(3 if section == 0 else 2):
                    part[m] += dot(x, w[pl.ds(m * RANK, RANK), at], NT)
                if section == 0:
                    u = w[pl.ds(0, RANK), at]
                    gram[0] += dot(u, u, NT)
                    gram[1] += dot(u, w[pl.ds(2 * RANK, RANK), at], NT)
                    xf = x.astype(F32)
                    sq[...] += jnp.broadcast_to(jnp.sum(xf * xf, axis=1, keepdims=True), sq.shape)

        local.wait()
        arrived(got, near, 0)
        first_sends(0)
        arrived(kept, far, 2)
        arrived(got, far, 1)
        first_sends(1)
        fill()
        part[...] = jnp.zeros_like(part)
        if section == 0:
            gram[...] = jnp.zeros_like(gram)
            sq[...] = jnp.zeros_like(sq)
        for r in range(2):
            came(spot(r, -1, 0), r, 0, 0)
            go(spot(r, -1, 0, halves[0]), r, 0, 2, along(r, 1, False))
            group_sends(r, 2)
            came(spot(r, 1, 0), r, 0, 1)
            go(spot(r, 1, 0, halves[1]), r, 0, 3, along(r, 3, False))
            group_sends(r, 3)
        pace()
        for r in range(2):
            forward(r, 1)
        for r in range(2):
            came(spot(r, 2, 0, halves[0]), r, 0, 2)
            came(spot(r, 2, 0, halves[1]), r, 0, 3)
            group_sends(r, 4)
        pace()
        filled()
        for g in (2, 3, 4):
            for r in range(2):
                forward(r, g)
            pace()
            for r in range(2):
                complete(r, g - 1)
            products(g - 1)
        for r in range(2):
            complete(r, 4)
        pace()
        products(4)

        to_core = [remote(part.at[:, other_rows], got_part, core_ss.at[0], core_rs.at[0], other_core)]
        if section == 0:
            to_core.append(remote(gram, got_gram, core_ss.at[1], core_rs.at[1], other_core))
            to_core.append(remote(sq.at[other_rows], got_sq, core_ss.at[2], core_rs.at[2], other_core))
        for copy in to_core:
            copy.start()
        for copy in to_core:
            copy.wait()
        for copy in started:
            copy.wait_send()
        return begun

    lr_mine, lr_other = lr.at[:, my_rows], lr.at[:, other_rows]
    bg_mine, bg_other = bg.at[:, my_rows], bg.at[:, other_rows]
    three = lr.at[pl.ds(0, 3), my_rows]
    three_other = lr.at[pl.ds(0, 3), other_rows]
    from_later = remote(sg, got_sg, sg_ss, sg_rs, later)

    @pl.when(s == 1)
    def _():
        begun = gather(1)
        sg[...] = part[pl.ds(0, 2), my_rows] + got_part[pl.ds(0, 2)]
        from_later.start()
        pl.loop(begun, 16)(exchange)
        from_later.wait_send()
        remote(three, three, lr_ss.at[0], lr_rs.at[0], later).wait_recv()
        hand_on = remote(three, three, lr_ss.at[1], lr_rs.at[1], other_core)
        hand_on.start()
        remote(three_other, three_other, lr_ss.at[1], lr_rs.at[1], other_core).wait_recv()
        hand_on.wait_send()
        lrt[0] = lr[1].astype(F32).T.astype(BF)
        lrt[1] = lr[2].astype(F32).T.astype(BF)

    @pl.when(s == 0)
    def _():
        begun = gather(0)
        q0, p0, r = [part[m, my_rows] + got_part[m] for m in range(3)]
        uu = gram[0] + got_gram[0]
        ua = gram[1] + got_gram[1]
        sx = (sq[my_rows] + got_sq[...])[:, :1]
        inv0 = lax.rsqrt(sx * (1.0 / D) + EPSILON)
        pre0 = p0 * inv0
        sig0 = 1.0 / (1.0 + jnp.exp(-pre0))
        act0 = (pre0 * sig0).astype(BF)
        act0f = act0.astype(F32)
        t = dot_wide(act0, uu, NN)
        sb = sx + jnp.sum(act0f * (2.0 * q0 + t), axis=1, keepdims=True)
        inv1 = lax.rsqrt(jnp.maximum(sb, 0.0) * (1.0 / D) + EPSILON)
        p1 = r + dot_wide(act0, ua, NN)
        pre1 = p1 * inv1
        sig1 = 1.0 / (1.0 + jnp.exp(-pre1))
        act1 = (pre1 * sig1).astype(BF)
        from_later.wait_recv()
        g0, g1 = got_sg[0], got_sg[1]
        pg1 = (g1 * sig1 * (1.0 + pre1 * (1.0 - sig1))).astype(BF).astype(F32)
        pg1s = (pg1 * inv1).astype(BF)
        lr[0, my_rows] = act0
        lr[1, my_rows] = pg1s
        lr[2, my_rows] = act1
        to_later = remote(three, three, lr_ss.at[0], lr_rs.at[0], later)
        to_later.start()
        pl.loop(begun, 16)(exchange)
        beta = inv1 * inv1 * inv1 * (jnp.sum(pg1 * p1, axis=1, keepdims=True) * (1.0 / D))
        ag0 = g0 + dot_wide(pg1s, ua, NT) - beta * (q0 + t)
        pg0 = (ag0 * sig0 * (1.0 + pre0 * (1.0 - sig0))).astype(BF).astype(F32)
        gamma = inv0 * inv0 * inv0 * (jnp.sum(pg0 * p0, axis=1, keepdims=True) * (1.0 / D))
        lr[3, my_rows] = (pg0 * inv0).astype(BF)
        bg[0, my_rows] = jnp.broadcast_to(beta, (ROWS, 128))
        bg[1, my_rows] = jnp.broadcast_to(gamma, (ROWS, 128))
        to_other = [
            remote(lr_mine, lr_mine, lr_ss.at[2], lr_rs.at[2], other_core),
            remote(bg_mine, bg_mine, lr_ss.at[3], lr_rs.at[3], other_core),
        ]
        for copy in to_other:
            copy.start()
        remote(lr_other, lr_other, lr_ss.at[2], lr_rs.at[2], other_core).wait_recv()
        remote(bg_other, bg_other, lr_ss.at[3], lr_rs.at[3], other_core).wait_recv()
        for copy in to_other:
            copy.wait_send()
        lrt[0] = lr[3].astype(F32).T.astype(BF)
        lrt[1] = lr[0].astype(F32).T.astype(BF)
        to_later.wait_send()

    top, bottom = pl.ds(0, RANK), pl.ds(RANK, RANK)

    def blocks(n):
        oa = FROM_BACK[n]

        @pl.loop(0, 8)
        def _(j):
            ob, r = away(j // 2), lax.rem(j, 2)
            at = lanes(r, oa, ob)
            a, b = place(r, oa, ob)
            here = pl.ds(pl.multiple_of(ob * BLK, BLK), BLK)
            new = oth.at[:, at]
            remote(new, new, ex_ss, ex_rs.at[n * 4 + j // 2, r], later).wait_recv()
            if oa in (1, 3):
                k, rows = (0, top) if oa == 1 else (1, bottom)
                src = r0.at[r, k, :, here]
                remote(src, src, p0_ss, p0_rs.at[r, k, ob], later).wait_recv()

            def store(down, up):
                if oa == 1:
                    down += r0[r, 0, :, here].astype(F32)
                if oa == 3:
                    up += r0[r, 1, :, here].astype(F32)
                gp[top, at] = down.astype(BF)
                gp[bottom, at] = up.astype(BF)

            @pl.when(s == 0)
            def _():
                x, g = own[:, at], oth[:, at]
                xf = x.astype(F32)
                beta = bg[0][:, :1]
                gamma = bg[1][:, :1]
                bound = (xf + dot(lr[0], w[pl.ds(0, RANK), at], NN)).astype(BF).astype(F32)
                passed = (g.astype(F32) + dot(lr[1], w[pl.ds(2 * RANK, RANK), at], NN) - beta * bound).astype(BF)
                out[:, at] = (passed.astype(F32) + dot(lr[3], w[pl.ds(RANK, RANK), at], NN) - gamma * xf).astype(BF)
                store(dot(lrt[0], x, NN), dot(lrt[1], passed, NN))

            @pl.when(s == 1)
            def _():
                x, g = oth[:, at], own[:, at]
                bound = (x.astype(F32) + dot(lr[0], w[pl.ds(0, RANK), at], NN)).astype(BF)
                out[:, at] = (bound.astype(F32) + dot(lr[2], w[pl.ds(RANK, RANK), at], NN)).astype(BF)
                store(dot(lrt[0], bound, NN), dot(lrt[1], g, NN))

            if oa == 2:
                for k, rows, d in ((0, top, 1), (1, bottom, 3)):
                    remote(gp.at[rows, at], r0.at[r, k, :, here], p0_ss, p0_rs.at[r, k, ob], along(r, d, False)).start()
            elif oa:
                k = 0 if oa == 1 else 1
                remote(gp.at[:, at], r1.at[r, k, :, here], p1_ss, p1_rs.at[r, k, ob], along(r, oa, False)).start()
            there = res.at[:, feed_at(r, a, b, c)]
            pltpu.make_async_copy(out.at[my_rows, at], there, out_ls).start()
            remote(out.at[other_rows, at], there, out_ss, out_rs, other_core).start()
            if oa == 0:
                total = gp[:, at].astype(F32)
                for k in range(2):
                    src = r1.at[r, k, :, here]
                    remote(src, src, p1_ss, p1_rs.at[r, k, ob], later).wait_recv()
                    total += src[...].astype(F32)

                @pl.when(ob == 0)
                def _():
                    tot[r] = total

                @pl.when(ob != 0)
                def _():
                    gp[:, at] = total.astype(BF)
                    remote(gp.at[:, at], r2.at[r, ob - 1], p2_ss, p2_rs.at[r, ob - 1], along(r, ob, True)).start()

    for n in range(4):
        blocks(n)

    def summed(r):
        total = tot[r]
        for k in range(3):
            remote(r2.at[r, k], r2.at[r, k], p2_ss, p2_rs.at[r, k], later).wait_recv()
            total += r2[r, k].astype(F32)
        return total

    send3[...] = summed(1).astype(BF)
    across = remote(send3, r3, p3_ss, p3_rs, dev(dx=1))
    across.start()
    total = summed(0)
    across.wait()
    wg[...] = total + r3[...].astype(F32)

    there = own.at[other_rows, :]
    remote(there, there, own_ss, own_rs, other_core).wait_send()
    remote(oth, oth, ex_ss, ex_rs.at[0, 0], later).wait_send()
    ref = gp.at[top, pl.ds(0, 16 * BLK)]
    remote(ref, ref, p0_ss, p0_rs.at[0, 0, 0], later).wait_send()
    ref = gp.at[:, pl.ds(0, 16 * BLK)]
    remote(ref, ref, p1_ss, p1_rs.at[0, 0, 0], later).wait_send()
    ref = gp.at[:, pl.ds(0, 6 * BLK)]
    remote(ref, ref, p2_ss, p2_rs.at[0, 0], later).wait_send()
    half = out.at[my_rows, :]
    pltpu.make_async_copy(half, half, out_ls).wait()
    remote(half, half, out_ss, out_rs, other_core).wait()


def per_device(section_feeds, adapter_weights):
    shard = adapter_weights[0]
    feed = section_feeds[0].reshape(ROWS, D)
    first = lax.axis_index("section") == 0
    down, up = shard[:, :RANK].T, shard[:, RANK:].T
    wt = jnp.where(first, jnp.concatenate([up, down]), jnp.concatenate([down, up]))
    dma = pltpu.SemaphoreType.DMA
    vm = pltpu.VMEM
    res, wg = pl.pallas_call(
        kernel,
        out_shape=(jax.ShapeDtypeStruct((ROWS, D), BF), jax.ShapeDtypeStruct((2 * RANK, BLK), F32)),
        in_specs=[pl.BlockSpec(memory_space=pl.ANY), pl.BlockSpec(memory_space=pltpu.VMEM)],
        out_specs=(pl.BlockSpec(memory_space=pl.ANY), pl.BlockSpec(memory_space=pltpu.VMEM)),
        scratch_shapes=[
            vm((2 * ROWS, HALF), BF), vm((2 * ROWS, HALF), BF), vm((3 * RANK, HALF), BF),
            vm((2 * ROWS, HALF), BF), vm((2 * RANK, HALF), BF),
            vm((2, 2, RANK, RING), BF), vm((2, 2, 2 * RANK, RING), BF), vm((2, 3, 2 * RANK, BLK), BF),
            vm((2, 2 * RANK, BLK), F32), vm((2 * RANK, BLK), BF), vm((2 * RANK, BLK), BF),
            vm((3, 2 * ROWS, RANK), F32), vm((2, RANK, RANK), F32), vm((2 * ROWS, 128), F32),
            vm((3, ROWS, RANK), F32), vm((2, RANK, RANK), F32), vm((ROWS, 128), F32),
            vm((2, ROWS, RANK), F32), vm((2, ROWS, RANK), F32),
            vm((4, 2 * ROWS, RANK), BF), vm((2, 2 * ROWS, 128), F32), vm((2, RANK, 2 * ROWS), BF),
            dma, dma, dma, dma, dma((16, 2)), dma((3,)), dma((3,)), dma,
            dma((2, 5, 4)), dma((2, 5, 4)), dma((3,)), dma((3,)), dma, dma, dma((4,)), dma((4,)),
            dma, dma((2, 2, 4)), dma, dma((2, 2, 4)), dma, dma((2, 3)), dma, dma, dma, dma, dma,
        ],
        compiler_params=pltpu.CompilerParams(
            collective_id=0, has_side_effects=True, vmem_limit_bytes=60 * 2**20),
        cost_estimate=pl.CostEstimate(flops=8 * 10**9, bytes_accessed=10**7, transcendentals=0),
        name="relay",
    )(feed, wt)
    return res.reshape(section_feeds.shape), wg.T.astype(BF)[None]


def solution(mesh):
    placed = (P("section", None, "fsdp", None), P("section", "fsdp", None))
    return jax.shard_map(per_device, mesh=mesh, in_specs=placed, out_specs=placed, check_vma=False)
```

time: 649 us -> 140 us (0.22); the launches traced: 640 us -> 140 us
  waiting for transfers between devices: 551 us -> 0 us
  Pallas kernels: 0 us -> 131 us
  matrix products: 41.7 us -> 0 us
  other arithmetic: 20.7 us -> 1.76 us
  between operations: 14.6 us -> 0.66 us
    reduce_scatter x1 -> x0, waiting for transfers between devices: 252 us -> none  [per_device(): lax.psum_scatter(jnp.concatenate([down_part, up_part], axis=1), 'fsdp', s...]
    ppermute x2 -> x0, waiting for transfers between devices: 201 us -> none  [from_behind(): lax.ppermute(value, axis, [(source, source + steps) for source in range(f...]
    pallas_call x0 -> x1, Pallas kernels: none -> 131 us  [per_device(): pl.pallas_call(kernel, out_shape=(jax.ShapeDtypeStruct((ROWS, D), BF), ja...]
    all_gather x1 -> x0, waiting for transfers between devices: 97.7 us -> none  [per_device(): weight_full = lax.all_gather(own_shard, 'fsdp', axis=0, tiled=True)]
    dot_general x6 -> x0, matrix products: 41.7 us -> none  [the longest x1 10.2 us: backward(): jnp.dot(upstream, weight_full[:, low_rank:], preferred_element_type=jnp.f...]
    concatenate x1 -> x0, other arithmetic: 8.71 us -> none  [per_device(): jnp.concatenate([down_part, up_part], axis=1)]
  transfers between devices with their start and end apart: 4 -> 0, of which waited for: 4 -> 0; matrix products, arithmetic and copies ran while one was open for 1% -> 0% of each run, Pallas kernels for 0% -> 0%
where the time goes in v2:
time: 140 us
  Pallas kernels  131 us (94%)
  local copies, waits for them, and re-layouts  6.46 us (5%)
  other arithmetic  1.76 us (1%)
    pallas_call x1, Pallas kernels, per_device(): pl.pallas_call(kernel, out_shape=(jax.ShapeDtypeStruct((ROWS, D), BF), ja...  131 us
    unnamed x3, local copies, waits for them, and re-layouts  6.45 us

profile of v2, /device:TPU:2, one launch (start us, length us, event | category | flops | bytes accessed | tf_op | source)
XLA Modules:
  0.0 139.7 jit_solution(15834346708707599522)
XLA Ops:
  0.6 1.1 copy.4
  1.7 0.7 maximum_select_fusion.wt
  2.5 130.8 %relay.1 = (bf16[128,16384]{1,0:T(8,128)(2,1)}, f32[384,256]{1,0:T(8,128)}) custom-call(bf16[128,16384]{1,0:T(8,128)(2,1)} %bitcast.13, bf16[384,256]{1,0:T(8,128)(2,1)} %maximum_select_fusion.wt), custom_call_target="tpu_custom_call" | custom-call | flops 8000000000 | bytes 10000000 | tf_op jit(solution)/shard_map/relay/pallas_call | solution.py:431
  133.3 1.0 convert_bitcast_fusion
  134.3 0.8 copy.5
  135.1 4.6 %copy.7 = bf16[1,2,64,16384]{3,2,1,0:T(8,128)(2,1)} copy(bf16[1,2,64,16384]{3,2,1,0:T(8,128)(2,1)} %bitcast.11) | data formatting | bytes 8388608
  (1 shorter events, 0.0 us)

commit v3 on v2

v3 whole, which is shorter than its diff:
```python
import jax
import jax.numpy as jnp
from jax import lax
from jax.experimental import pallas as pl
from jax.experimental.pallas import tpu as pltpu
from jax.sharding import PartitionSpec as P

MESH = pl.DeviceIdType.MESH
EPSILON = 1e-05
BF = jnp.bfloat16
F32 = jnp.float32
NT = (((1,), (1,)), ((), ()))
NN = (((1,), (0,)), ((), ()))
D = 16384
RANK = 192
ROWS = 128
HALF = D // 2
BLK = 256
RING = 4 * BLK
PACE = ((2, 4, 5, 6, 7, 8, 9), (3, 5, 6, 7, 8, 9, 9))
FROM_BACK = (2, 3, 1, 0)


def dot(a, b, dims):
    return lax.dot_general(a, b, dims, preferred_element_type=F32)


def dot_wide(a, b, dims):
    high = b.astype(BF)
    low = (b - high.astype(F32)).astype(BF)
    return dot(a, high, dims) + dot(a, low, dims)


def away(i):
    return lax.rem(2 + (i * (i + 1)) // 2, 4)


def kernel(
    feed, shard, res, wg,
    own, oth, w, out, gp, r0, r1, r2, tot, send3, r3,
    part, gram, sq, got_part, got_gram, got_sq, sg, got_sg, lr, bg, lrt,
    own_ss, own_rs, own_ls, ex_ss, ex_rs, pre_ss, pre_rs,
    ag_ss, ag_rs, own_part_ss, ship_ss, ship_rs, core_ss, core_rs, sg_ss, sg_rs, lr_ss, lr_rs,
    p0_ss, p0_rs, p1_ss, p1_rs, p2_ss, p2_rs, p3_ss, p3_rs, out_ss, out_rs, out_ls,
):
    s = lax.axis_index("section")
    f = lax.axis_index("fsdp")
    c = lax.rem(f, 2)
    xh = lax.rem(f // 2, 2)
    y = lax.rem(f // 4, 4)
    z = f // 16

    def dev(ss=0, dx=0, dy=0, dz=0, dc=0):
        sx = lax.rem(s + ss, 2)
        at = (lax.rem(z + dz, 4) * 4 + lax.rem(y + dy, 4)) * 2 + lax.rem(xh + dx, 2)
        return (sx, at * 2 + lax.rem(c + dc, 2))

    def remote(src, dst, ssem, rsem, to):
        return pltpu.make_async_remote_copy(
            src_ref=src, dst_ref=dst, send_sem=ssem, recv_sem=rsem,
            device_id=to, device_id_type=MESH)

    other_core, later = dev(dc=1), dev(ss=1)

    def turned(r, core):
        return lax.rem(r + core, 2)

    def place(r, oa, ob, core=c):
        q = turned(r, core)
        pa, pb = y * (1 - q) + z * q, z * (1 - q) + y * q
        return lax.rem(pa + oa, 4), lax.rem(pb + ob, 4)

    def block(r, a, b):
        return pl.ds(pl.multiple_of(((r * 4 + a) * 4 + b) * BLK, BLK), BLK)

    def lanes(r, oa, ob):
        return block(r, *place(r, oa, ob))

    def group_lanes(r, oa):
        a, _ = place(r, oa, 0)
        return pl.ds(pl.multiple_of((r * 4 + a) * RING, RING), RING)

    def feed_at(r, a, b, core):
        q = turned(r, core)
        jj = (b * (1 - q) + a * q) * 4 + a * (1 - q) + b * q
        return pl.ds(pl.multiple_of(((jj * 2 + lax.rem(xh + r, 2)) * 2 + core) * BLK, BLK), BLK)

    def along(r, d, second):
        q = turned(r + int(second), c)
        return dev(dy=d * (1 - q), dz=d * q)

    peers = [dict(dc=1), dict(ss=1), dict(ss=1, dc=1), dict(dx=1), dict(ss=1, dx=1)]
    peers += [dict(dy=d) for d in (1, 2, 3)] + [dict(dz=d) for d in (1, 2, 3)]
    barrier = pltpu.get_barrier_semaphore()
    for peer in peers:
        pl.semaphore_signal(barrier, inc=1, device_id=dev(**peer), device_id_type=MESH)
    turned_shard = shard[...].astype(F32).T.astype(BF)

    @pl.when(s == 0)
    def _():
        w[pl.ds(0, RANK), lanes(0, 0, 0)] = turned_shard[RANK:]
        w[pl.ds(RANK, RANK), lanes(0, 0, 0)] = turned_shard[:RANK]

    @pl.when(s == 1)
    def _():
        w[pl.ds(2 * RANK, RANK), lanes(0, 0, 0)] = turned_shard[:RANK]
        w[pl.ds(RANK, RANK), lanes(0, 0, 0)] = turned_shard[RANK:]

    pl.semaphore_wait(barrier, len(peers))

    my_rows = pl.ds(pl.multiple_of(c * ROWS, ROWS), ROWS)
    other_rows = pl.ds(pl.multiple_of((1 - c) * ROWS, ROWS), ROWS)

    def exchange(i):
        for r in range(2):
            oa, ob = away(i // 4), away(lax.rem(i, 4))
            for dc in range(2):
                core = lax.rem(c + dc, 2)
                a, b = place(r, oa, ob, core)
                remote(
                    feed.at[:, feed_at(r, a, b, core)], oth.at[my_rows, block(r, a, b)],
                    ex_ss, ex_rs.at[i, r], dev(ss=1, dc=dc)).start()

    def fill():
        @pl.loop(0, 32)
        def _(k):
            r, a, b = k // 16, lax.rem(k // 4, 4), lax.rem(k, 4)
            at = pl.ds(pl.multiple_of(k * BLK, BLK), BLK)
            remote(feed.at[:, feed_at(r, a, b, 1 - c)], own.at[my_rows, at], own_ss, own_rs, other_core).start()
            pltpu.make_async_copy(feed.at[:, feed_at(r, a, b, c)], own.at[my_rows, at], own_ls).start()

    def filled():
        whole = own.at[my_rows, :]
        pltpu.make_async_copy(whole, whole, own_ls).wait()
        there = own.at[other_rows, :]
        remote(there, there, own_ss, own_rs, other_core).wait_recv()

    def gather(section):
        rows = (3 * RANK, 2 * RANK)
        halves = [(pl.ds(0, n // 2), pl.ds(n // 2, n // 2)) for n in rows]
        begun = 0
        points = iter(PACE[section])

        def pace():
            nonlocal begun
            upto = next(points)
            if upto > begun:
                pl.loop(begun, upto)(exchange)
            begun = upto

        near, far = lanes(0, 0, 0), lanes(1, 0, 0)
        first, both = pl.ds(0, RANK), pl.ds(0, 2 * RANK)
        middle, last = pl.ds(RANK, RANK), pl.ds(2 * RANK, RANK)
        sent, kept = (first, both) if section == 0 else (last, middle)
        got = last if section == 0 else first
        diagonal = dev(ss=1, dx=1)
        pre = [
            remote(w.at[sent, near], w.at[sent, near], pre_ss.at[0], pre_rs.at[0], later),
            remote(w.at[kept, near], w.at[kept, far], pre_ss.at[2], pre_rs.at[2], dev(dx=1)),
        ]
        if section == 0:
            pre.append(remote(w.at[first, near], w.at[first, far], pre_ss.at[1], pre_rs.at[1], diagonal))
        for copy in pre:
            copy.start()

        def arrived(rows, at, k):
            remote(w.at[rows, at], w.at[rows, at], pre_ss.at[k], pre_rs.at[k], later).wait_recv()

        def spot(r, oa, ob, part_rows=None):
            return w.at[pl.ds(0, rows[r]) if part_rows is None else part_rows, lanes(r, oa % 4, ob % 4)]

        started = list(pre)

        def go(ref, r, g, k, to, sem=None):
            copy = remote(ref, ref, ag_ss.at[r, g, k] if sem is None else sem, ag_rs.at[r, g, k], to)
            copy.start()
            started.append(copy)

        def came(ref, r, g, k):
            remote(ref, ref, ag_ss.at[r, g, k], ag_rs.at[r, g, k], later).wait_recv()

        order = (0, -1, 1, 2)

        def ship(oa, ob, half=None):
            if section == 0:
                return
            a, b = place(0, oa % 4, ob % 4)
            copy = remote(
                w.at[last, block(0, a, b)], w.at[last, block(1, b, a)], ship_ss.at[a * 4 + b], ship_rs.at[b * 4 + a],
                diagonal)
            copy.start()
            started.append(copy)

        def group_sends(r, g):
            for k, d in ((0, 1), (1, 3)):
                go(spot(r, order[g - 1], 0), r, g, k, along(r, d, True))

        def first_sends(r):
            for k, d in ((0, 1), (1, 3)):
                go(spot(r, 0, 0), r, 0, k, along(r, d, False))
            group_sends(r, 1)

        def forward(r, g):
            oa = order[g - 1]
            for k, d in ((0, -1), (1, 1)):
                came(spot(r, oa, d), r, g, k)
                go(spot(r, oa, d, halves[r][k]), r, g, 2 + k, along(r, -d % 4, True))
                if r == 0:
                    ship(oa, d)

        def complete(r, g):
            oa = order[g - 1]
            came(spot(r, oa, 2, halves[r][0]), r, g, 2)
            came(spot(r, oa, 2, halves[r][1]), r, g, 3)
            if r == 0:
                ship(oa, 2)

        def products(g):
            for r in range(2):
                at = group_lanes(r, order[g - 1] % 4)
                x = own[:, at]
                wide = section == 0 and r == 0
                for m in range(3 if wide else 2):
                    part[m] += dot(x, w[pl.ds(m * RANK, RANK), at], NT)
                if section == 0:
                    u = w[pl.ds(0, RANK), at]
                    gram[0] += dot(u, u, NT)
                    if wide:
                        gram[1] += dot(u, w[last, at], NT)
                    xf = x.astype(F32)
                    sq[...] += jnp.broadcast_to(jnp.sum(xf * xf, axis=1, keepdims=True), sq.shape)

        def far_products():
            for k in range(16):
                ref = w.at[last, pl.ds((16 + k) * BLK, BLK)]
                remote(ref, ref, ship_ss.at[0], ship_rs.at[k], diagonal).wait_recv()

            @pl.loop(0, 4)
            def _(k):
                at = pl.ds(pl.multiple_of((4 + k) * RING, RING), RING)
                part[2] += dot(own[:, at], w[last, at], NT)
                gram[1] += dot(w[pl.ds(0, RANK), at], w[last, at], NT)

        local = both if section == 0 else pl.ds(RANK, 2 * RANK)
        for rows_now, sem in ((local, own_part_ss), (got, None)):
            if sem is None:
                ship(0, 0)
                pace()
                arrived(got, near, 0)
            for second in (False, True):
                for k, d in ((0, 1), (1, 3)):
                    go(spot(0, 0, 0, rows_now), 0, int(second), k, along(0, d, second),
                       None if sem is None else sem.at[int(second), k])
        arrived(kept, far, 2)
        if section == 1:
            arrived(got, far, 1)
        first_sends(1)
        fill()
        part[...] = jnp.zeros_like(part)
        if section == 0:
            gram[...] = jnp.zeros_like(gram)
            sq[...] = jnp.zeros_like(sq)
        for r in range(2):
            for k, d in ((0, -1), (1, 1)):
                came(spot(r, d, 0), r, 0, k)
                go(spot(r, d, 0, halves[r][k]), r, 0, 2 + k, along(r, -d % 4, False))
                group_sends(r, 2 + k)
                if r == 0:
                    ship(d, 0)
        pace()
        for r in range(2):
            forward(r, 1)
        for r in range(2):
            came(spot(r, 2, 0, halves[r][0]), r, 0, 2)
            came(spot(r, 2, 0, halves[r][1]), r, 0, 3)
            group_sends(r, 4)
            if r == 0:
                ship(2, 0)
        pace()
        filled()
        for g in (2, 3, 4):
            for r in range(2):
                forward(r, g)
            pace()
            if g == 3:
                for r in range(2):
                    complete(r, 1)
                products(1)
        for g in (2, 3):
            for r in range(2):
                complete(r, g)
            products(g)
        for r in range(2):
            complete(r, 4)
        pace()
        products(4)

        def to_core(src, dst, k):
            copy = remote(src, dst, core_ss.at[k], core_rs.at[k], other_core)
            copy.start()
            return copy

        two, third = pl.ds(0, 2), pl.ds(2, 1)
        handed = [to_core(part.at[two, other_rows], got_part.at[two], 0)]
        if section == 0:
            handed.append(to_core(gram.at[0], got_gram.at[0], 1))
            handed.append(to_core(sq.at[other_rows], got_sq, 2))
            far_products()
            handed.append(to_core(part.at[third, other_rows], got_part.at[third], 3))
            handed.append(to_core(gram.at[1], got_gram.at[1], 4))
        for copy in handed:
            copy.wait()
        return begun, started

    lr_mine, lr_other = lr.at[:, my_rows], lr.at[:, other_rows]
    bg_mine, bg_other = bg.at[:, my_rows], bg.at[:, other_rows]
    three = lr.at[pl.ds(0, 3), my_rows]
    three_other = lr.at[pl.ds(0, 3), other_rows]
    from_later = remote(sg, got_sg, sg_ss, sg_rs, later)

    @pl.when(s == 1)
    def _():
        begun, started = gather(1)
        sg[...] = part[pl.ds(0, 2), my_rows] + got_part[pl.ds(0, 2)]
        from_later.start()
        pl.loop(begun, 16)(exchange)
        from_later.wait_send()
        remote(three, three, lr_ss.at[0], lr_rs.at[0], later).wait_recv()
        hand_on = remote(three, three, lr_ss.at[1], lr_rs.at[1], other_core)
        hand_on.start()
        remote(three_other, three_other, lr_ss.at[1], lr_rs.at[1], other_core).wait_recv()
        hand_on.wait_send()
        for copy in started:
            copy.wait_send()
        lrt[0] = lr[1].astype(F32).T.astype(BF)
        lrt[1] = lr[2].astype(F32).T.astype(BF)

    @pl.when(s == 0)
    def _():
        begun, started = gather(0)
        q0, p0, r = [part[m, my_rows] + got_part[m] for m in range(3)]
        uu = gram[0] + got_gram[0]
        ua = gram[1] + got_gram[1]
        sx = (sq[my_rows] + got_sq[...])[:, :1]
        inv0 = lax.rsqrt(sx * (1.0 / D) + EPSILON)
        pre0 = p0 * inv0
        sig0 = 1.0 / (1.0 + jnp.exp(-pre0))
        act0 = (pre0 * sig0).astype(BF)
        act0f = act0.astype(F32)
        t = dot_wide(act0, uu, NN)
        sb = sx + jnp.sum(act0f * (2.0 * q0 + t), axis=1, keepdims=True)
        inv1 = lax.rsqrt(jnp.maximum(sb, 0.0) * (1.0 / D) + EPSILON)
        p1 = r + dot_wide(act0, ua, NN)
        pre1 = p1 * inv1
        sig1 = 1.0 / (1.0 + jnp.exp(-pre1))
        act1 = (pre1 * sig1).astype(BF)
        from_later.wait_recv()
        g0, g1 = got_sg[0], got_sg[1]
        pg1 = (g1 * sig1 * (1.0 + pre1 * (1.0 - sig1))).astype(BF).astype(F32)
        pg1s = (pg1 * inv1).astype(BF)
        lr[0, my_rows] = act0
        lr[1, my_rows] = pg1s
        lr[2, my_rows] = act1
        to_later = remote(three, three, lr_ss.at[0], lr_rs.at[0], later)
        to_later.start()
        pl.loop(begun, 16)(exchange)
        beta = inv1 * inv1 * inv1 * (jnp.sum(pg1 * p1, axis=1, keepdims=True) * (1.0 / D))
        ag0 = g0 + dot_wide(pg1s, ua, NT) - beta * (q0 + t)
        pg0 = (ag0 * sig0 * (1.0 + pre0 * (1.0 - sig0))).astype(BF).astype(F32)
        gamma = inv0 * inv0 * inv0 * (jnp.sum(pg0 * p0, axis=1, keepdims=True) * (1.0 / D))
        lr[3, my_rows] = (pg0 * inv0).astype(BF)
        bg[0, my_rows] = jnp.broadcast_to(beta, (ROWS, 128))
        bg[1, my_rows] = jnp.broadcast_to(gamma, (ROWS, 128))
        to_other = [
            remote(lr_mine, lr_mine, lr_ss.at[2], lr_rs.at[2], other_core),
            remote(bg_mine, bg_mine, lr_ss.at[3], lr_rs.at[3], other_core),
        ]
        for copy in to_other:
            copy.start()
        remote(lr_other, lr_other, lr_ss.at[2], lr_rs.at[2], other_core).wait_recv()
        remote(bg_other, bg_other, lr_ss.at[3], lr_rs.at[3], other_core).wait_recv()
        for copy in to_other + started:
            copy.wait_send()
        lrt[0] = lr[3].astype(F32).T.astype(BF)
        lrt[1] = lr[0].astype(F32).T.astype(BF)
        to_later.wait_send()

    top, bottom = pl.ds(0, RANK), pl.ds(RANK, RANK)

    def blocks(n):
        oa = FROM_BACK[n]

        @pl.loop(0, 4)
        def _(j):
            ob = away(j)
            here = pl.ds(pl.multiple_of(ob * BLK, BLK), BLK)
            both = range(2)
            at = [lanes(r, oa, ob) for r in both]
            for r in both:
                new = oth.at[:, at[r]]
                remote(new, new, ex_ss, ex_rs.at[n * 4 + j, r], later).wait_recv()
                if oa in (1, 3):
                    k = oa // 2
                    src = r0.at[r, k, :, here]
                    remote(src, src, p0_ss, p0_rs.at[r, k, ob], later).wait_recv()

            def store(done, down, up):
                if oa == 1:
                    down = [down[r] + r0[r, 0, :, here].astype(F32) for r in both]
                if oa == 3:
                    up = [up[r] + r0[r, 1, :, here].astype(F32) for r in both]
                for r in both:
                    out[:, at[r]] = done[r]
                    gp[top, at[r]] = down[r].astype(BF)
                    gp[bottom, at[r]] = up[r].astype(BF)

            @pl.when(s == 0)
            def _():
                x, g = [own[:, at[r]] for r in both], [oth[:, at[r]] for r in both]
                xf = [x[r].astype(F32) for r in both]
                beta = bg[0][:, :1]
                gamma = bg[1][:, :1]
                grown = [dot(lr[0], w[pl.ds(0, RANK), at[r]], NN) for r in both]
                slope = [dot(lr[1], w[pl.ds(2 * RANK, RANK), at[r]], NN) for r in both]
                bound = [(xf[r] + grown[r]).astype(BF).astype(F32) for r in both]
                passed = [(g[r].astype(F32) + slope[r] - beta * bound[r]).astype(BF) for r in both]
                first = [dot(lr[3], w[pl.ds(RANK, RANK), at[r]], NN) for r in both]
                down = [dot(lrt[0], x[r], NN) for r in both]
                up = [dot(lrt[1], passed[r], NN) for r in both]
                done = [(passed[r].astype(F32) + first[r] - gamma * xf[r]).astype(BF) for r in both]
                store(done, down, up)

            @pl.when(s == 1)
            def _():
                x, g = [oth[:, at[r]] for r in both], [own[:, at[r]] for r in both]
                grown = [dot(lr[0], w[pl.ds(0, RANK), at[r]], NN) for r in both]
                final = [dot(lr[2], w[pl.ds(RANK, RANK), at[r]], NN) for r in both]
                up = [dot(lrt[1], g[r], NN) for r in both]
                bound = [(x[r].astype(F32) + grown[r]).astype(BF) for r in both]
                down = [dot(lrt[0], bound[r], NN) for r in both]
                done = [(bound[r].astype(F32) + final[r]).astype(BF) for r in both]
                store(done, down, up)

            for r in both:
                if oa == 2:
                    for k, rows, d in ((0, top, 1), (1, bottom, 3)):
                        remote(
                            gp.at[rows, at[r]], r0.at[r, k, :, here], p0_ss, p0_rs.at[r, k, ob],
                            along(r, d, False)).start()
                elif oa:
                    k = oa // 2
                    remote(
                        gp.at[:, at[r]], r1.at[r, k, :, here], p1_ss, p1_rs.at[r, k, ob], along(r, oa, False)).start()
            for r in both:
                there = res.at[:, feed_at(r, *place(r, oa, ob), c)]
                pltpu.make_async_copy(out.at[my_rows, at[r]], there, out_ls).start()
                remote(out.at[other_rows, at[r]], there, out_ss, out_rs, other_core).start()
            if oa == 0:
                for r in both:
                    total = gp[:, at[r]].astype(F32)
                    for k in range(2):
                        src = r1.at[r, k, :, here]
                        remote(src, src, p1_ss, p1_rs.at[r, k, ob], later).wait_recv()
                        total += src[...].astype(F32)

                    @pl.when(ob == 0)
                    def _():
                        tot[r] = total

                    @pl.when(ob != 0)
                    def _():
                        gp[:, at[r]] = total.astype(BF)
                        remote(
                            gp.at[:, at[r]], r2.at[r, ob - 1], p2_ss, p2_rs.at[r, ob - 1], along(r, ob, True)).start()

    for n in range(4):
        blocks(n)

    def summed(r):
        total = tot[r]
        for k in range(3):
            remote(r2.at[r, k], r2.at[r, k], p2_ss, p2_rs.at[r, k], later).wait_recv()
            total += r2[r, k].astype(F32)
        return total

    send3[...] = summed(1).astype(BF)
    across = remote(send3, r3, p3_ss, p3_rs, dev(dx=1))
    across.start()
    total = summed(0)
    across.wait()
    wg[...] = (total + r3[...].astype(F32)).T.astype(BF)

    there = own.at[other_rows, :]
    remote(there, there, own_ss, own_rs, other_core).wait_send()
    remote(oth, oth, ex_ss, ex_rs.at[0, 0], later).wait_send()
    ref = gp.at[top, pl.ds(0, 16 * BLK)]
    remote(ref, ref, p0_ss, p0_rs.at[0, 0, 0], later).wait_send()
    ref = gp.at[:, pl.ds(0, 16 * BLK)]
    remote(ref, ref, p1_ss, p1_rs.at[0, 0, 0], later).wait_send()
    ref = gp.at[:, pl.ds(0, 6 * BLK)]
    remote(ref, ref, p2_ss, p2_rs.at[0, 0], later).wait_send()
    half = out.at[my_rows, :]
    pltpu.make_async_copy(half, half, out_ls).wait()
    remote(half, half, out_ss, out_rs, other_core).wait()


def per_device(section_feeds, adapter_weights):
    shard = adapter_weights[0]
    feed = section_feeds[0].reshape(ROWS, D)
    dma = pltpu.SemaphoreType.DMA
    vm = pltpu.VMEM
    res, wg = pl.pallas_call(
        kernel,
        out_shape=(jax.ShapeDtypeStruct((ROWS, D), BF), jax.ShapeDtypeStruct((BLK, 2 * RANK), BF)),
        in_specs=[pl.BlockSpec(memory_space=pl.ANY), pl.BlockSpec(memory_space=pltpu.VMEM)],
        out_specs=(pl.BlockSpec(memory_space=pl.ANY), pl.BlockSpec(memory_space=pltpu.VMEM)),
        scratch_shapes=[
            vm((2 * ROWS, HALF), BF), vm((2 * ROWS, HALF), BF), vm((3 * RANK, HALF), BF),
            vm((2 * ROWS, HALF), BF), vm((2 * RANK, HALF), BF),
            vm((2, 2, RANK, RING), BF), vm((2, 2, 2 * RANK, RING), BF), vm((2, 3, 2 * RANK, BLK), BF),
            vm((2, 2 * RANK, BLK), F32), vm((2 * RANK, BLK), BF), vm((2 * RANK, BLK), BF),
            vm((3, 2 * ROWS, RANK), F32), vm((2, RANK, RANK), F32), vm((2 * ROWS, 128), F32),
            vm((3, ROWS, RANK), F32), vm((2, RANK, RANK), F32), vm((ROWS, 128), F32),
            vm((2, ROWS, RANK), F32), vm((2, ROWS, RANK), F32),
            vm((4, 2 * ROWS, RANK), BF), vm((2, 2 * ROWS, 128), F32), vm((2, RANK, 2 * ROWS), BF),
            dma, dma, dma, dma, dma((16, 2)), dma((3,)), dma((3,)),
            dma((2, 5, 4)), dma((2, 5, 4)), dma((2, 2)), dma((16,)), dma((16,)), dma((5,)), dma((5,)), dma, dma, dma((4,)), dma((4,)),
            dma, dma((2, 2, 4)), dma, dma((2, 2, 4)), dma, dma((2, 3)), dma, dma, dma, dma, dma,
        ],
        compiler_params=pltpu.CompilerParams(
            collective_id=0, has_side_effects=True, vmem_limit_bytes=60 * 2**20),
        cost_estimate=pl.CostEstimate(flops=8 * 10**9, bytes_accessed=10**7, transcendentals=0),
        name="relay",
    )(feed, shard)
    return res.reshape(section_feeds.shape), wg[None]


def solution(mesh):
    placed = (P("section", None, "fsdp", None), P("section", "fsdp", None))
    return jax.shard_map(per_device, mesh=mesh, in_specs=placed, out_specs=placed, check_vma=False)
```

time: 140 us -> 134 us (0.957)
  Pallas kernels: 131 us -> 128 us
  other arithmetic: 1.76 us -> 0 us
    pallas_call x1, Pallas kernels: 131 us -> 128 us  [per_device(): pl.pallas_call(kernel, out_shape=(jax.ShapeDtypeStruct((ROWS, D), BF), ja...]
    unnamed x3 -> x4, local copies, waits for them, and re-layouts: 6.45 us -> 5.29 us
where the time goes in v3:
time: 134 us
  Pallas kernels  128 us (96%)
  local copies, waits for them, and re-layouts  5.29 us (4%)
    pallas_call x1, Pallas kernels, per_device(): pl.pallas_call(kernel, out_shape=(jax.ShapeDtypeStruct((ROWS, D), BF), ja...  128 us
    unnamed x4, local copies, waits for them, and re-layouts  5.29 us

profile of v3, /device:TPU:2, one launch (start us, length us, event | category | flops | bytes accessed | tf_op | source)
XLA Modules:
  0.0 134.2 jit_solution(2845476016254056072)
XLA Ops:
  0.6 128.2 %relay.1 = (bf16[128,16384]{1,0:T(8,128)(2,1)}, bf16[256,384]{1,0:T(8,128)(2,1)}) custom-call(bf16[128,16384]{1,0:T(8,128)(2,1)} %bitcast.6, bf16[256,384]{1,0:T(8,128)(2,1)} %bitcast.7), custom_call_target="tpu_custom_call" | custom-call | flops 8000000000 | bytes 10000000 | tf_op jit(solution)/shard_map/relay/pallas_call | solution.py:512
  128.9 0.0 copy-start
  128.9 4.6 %copy.6 = bf16[1,2,64,16384]{3,2,1,0:T(8,128)(2,1)} copy(bf16[1,2,64,16384]{3,2,1,0:T(8,128)(2,1)} %bitcast.4) | data formatting | bytes 8388608
  133.5 0.0 copy-done
  133.5 0.7 copy.7
Async XLA Ops:
  128.9 4.6 %copy-start = (bf16[256,384]{1,0:T(8,128)(2,1)S(1)}, bf16[256,384]{1,0:T(8,128)(2,1)}, u32[]{:S(2)}) copy-start(bf16[256,384]{1,0:T(8,128)(2,1)} %get-tuple-element.5) | copy-start | bytes 589828

commit v4 on v3

--- a/solution.py
+++ b/solution.py
@@ -17,7 +17,7 @@
 HALF = D // 2
 BLK = 256
 RING = 4 * BLK
-PACE = ((2, 4, 5, 6, 7, 8, 9), (3, 5, 6, 7, 8, 9, 9))
+PACE = ((2, 4, 5, 6, 7, 8, 9), (2, 4, 5, 5, 6, 7, 8, 9))
 FROM_BACK = (2, 3, 1, 0)
 
 
@@ -135,9 +135,11 @@
         there = own.at[other_rows, :]
         remote(there, there, own_ss, own_rs, other_core).wait_recv()
 
+    from_later = [remote(sg.at[m], got_sg.at[m], sg_ss.at[m], sg_rs.at[m], later) for m in range(2)]
+
     def gather(section):
-        rows = (3 * RANK, 2 * RANK)
-        halves = [(pl.ds(0, n // 2), pl.ds(n // 2, n // 2)) for n in rows]
+        rows = [(0, 3 * RANK), (0, 2 * RANK) if section == 0 else (RANK, RANK)]
+        halves = [(pl.ds(start, n // 2), pl.ds(start + n // 2, n // 2)) for start, n in rows]
         begun = 0
         points = iter(PACE[section])
 
@@ -158,8 +160,6 @@
             remote(w.at[sent, near], w.at[sent, near], pre_ss.at[0], pre_rs.at[0], later),
             remote(w.at[kept, near], w.at[kept, far], pre_ss.at[2], pre_rs.at[2], dev(dx=1)),
         ]
-        if section == 0:
-            pre.append(remote(w.at[first, near], w.at[first, far], pre_ss.at[1], pre_rs.at[1], diagonal))
         for copy in pre:
             copy.start()
 
@@ -167,7 +167,7 @@
             remote(w.at[rows, at], w.at[rows, at], pre_ss.at[k], pre_rs.at[k], later).wait_recv()
 
         def spot(r, oa, ob, part_rows=None):
-            return w.at[pl.ds(0, rows[r]) if part_rows is None else part_rows, lanes(r, oa % 4, ob % 4)]
+            return w.at[pl.ds(*rows[r]) if part_rows is None else part_rows, lanes(r, oa % 4, ob % 4)]
 
         started = list(pre)
 
@@ -181,12 +181,10 @@
 
         order = (0, -1, 1, 2)
 
-        def ship(oa, ob, half=None):
-            if section == 0:
-                return
+        def ship(oa, ob):
             a, b = place(0, oa % 4, ob % 4)
             copy = remote(
-                w.at[last, block(0, a, b)], w.at[last, block(1, b, a)], ship_ss.at[a * 4 + b], ship_rs.at[b * 4 + a],
+                w.at[sent, block(0, a, b)], w.at[sent, block(1, b, a)], ship_ss.at[a * 4 + b], ship_rs.at[b * 4 + a],
                 diagonal)
             copy.start()
             started.append(copy)
@@ -220,7 +218,7 @@
                 at = group_lanes(r, order[g - 1] % 4)
                 x = own[:, at]
                 wide = section == 0 and r == 0
-                for m in range(3 if wide else 2):
+                for m in range(3 if wide else 2) if section == 0 or r == 0 else (1,):
                     part[m] += dot(x, w[pl.ds(m * RANK, RANK), at], NT)
                 if section == 0:
                     u = w[pl.ds(0, RANK), at]
@@ -232,14 +230,15 @@
 
         def far_products():
             for k in range(16):
-                ref = w.at[last, pl.ds((16 + k) * BLK, BLK)]
+                ref = w.at[got, pl.ds((16 + k) * BLK, BLK)]
                 remote(ref, ref, ship_ss.at[0], ship_rs.at[k], diagonal).wait_recv()
 
             @pl.loop(0, 4)
             def _(k):
                 at = pl.ds(pl.multiple_of((4 + k) * RING, RING), RING)
-                part[2] += dot(own[:, at], w[last, at], NT)
-                gram[1] += dot(w[pl.ds(0, RANK), at], w[last, at], NT)
+                part[2 if section == 0 else 0] += dot(own[:, at], w[got, at], NT)
+                if section == 0:
+                    gram[1] += dot(w[pl.ds(0, RANK), at], w[last, at], NT)
 
         local = both if section == 0 else pl.ds(RANK, 2 * RANK)
         for rows_now, sem in ((local, own_part_ss), (got, None)):
@@ -252,8 +251,6 @@
                     go(spot(0, 0, 0, rows_now), 0, int(second), k, along(0, d, second),
                        None if sem is None else sem.at[int(second), k])
         arrived(kept, far, 2)
-        if section == 1:
-            arrived(got, far, 1)
         first_sends(1)
         fill()
         part[...] = jnp.zeros_like(part)
@@ -300,31 +297,39 @@
             copy.start()
             return copy
 
-        two, third = pl.ds(0, 2), pl.ds(2, 1)
-        handed = [to_core(part.at[two, other_rows], got_part.at[two], 0)]
         if section == 0:
-            handed.append(to_core(gram.at[0], got_gram.at[0], 1))
-            handed.append(to_core(sq.at[other_rows], got_sq, 2))
+            two, third = pl.ds(0, 2), pl.ds(2, 1)
+            handed = [
+                to_core(part.at[two, other_rows], got_part.at[two], 0),
+                to_core(gram.at[0], got_gram.at[0], 1),
+                to_core(sq.at[other_rows], got_sq, 2),
+            ]
             far_products()
             handed.append(to_core(part.at[third, other_rows], got_part.at[third], 3))
             handed.append(to_core(gram.at[1], got_gram.at[1], 4))
-        for copy in handed:
-            copy.wait()
+            for copy in handed:
+                copy.wait()
+        else:
+            for m, k in ((1, 0), (0, 3)):
+                if m == 0:
+                    pace()
+                    far_products()
+                to_core(part.at[pl.ds(m, 1), other_rows], got_part.at[pl.ds(m, 1)], k).wait()
+                sg[m] = part[m, my_rows] + got_part[m]
+                from_later[m].start()
         return begun, started
 
     lr_mine, lr_other = lr.at[:, my_rows], lr.at[:, other_rows]
     bg_mine, bg_other = bg.at[:, my_rows], bg.at[:, other_rows]
     three = lr.at[pl.ds(0, 3), my_rows]
     three_other = lr.at[pl.ds(0, 3), other_rows]
-    from_later = remote(sg, got_sg, sg_ss, sg_rs, later)
 
     @pl.when(s == 1)
     def _():
         begun, started = gather(1)
-        sg[...] = part[pl.ds(0, 2), my_rows] + got_part[pl.ds(0, 2)]
-        from_later.start()
         pl.loop(begun, 16)(exchange)
-        from_later.wait_send()
+        for copy in from_later:
+            copy.wait_send()
         remote(three, three, lr_ss.at[0], lr_rs.at[0], later).wait_recv()
         hand_on = remote(three, three, lr_ss.at[1], lr_rs.at[1], other_core)
         hand_on.start()
@@ -354,9 +359,8 @@
         pre1 = p1 * inv1
         sig1 = 1.0 / (1.0 + jnp.exp(-pre1))
         act1 = (pre1 * sig1).astype(BF)
-        from_later.wait_recv()
-        g0, g1 = got_sg[0], got_sg[1]
-        pg1 = (g1 * sig1 * (1.0 + pre1 * (1.0 - sig1))).astype(BF).astype(F32)
+        from_later[1].wait_recv()
+        pg1 = (got_sg[1] * sig1 * (1.0 + pre1 * (1.0 - sig1))).astype(BF).astype(F32)
         pg1s = (pg1 * inv1).astype(BF)
         lr[0, my_rows] = act0
         lr[1, my_rows] = pg1s
@@ -365,7 +369,8 @@
         to_later.start()
         pl.loop(begun, 16)(exchange)
         beta = inv1 * inv1 * inv1 * (jnp.sum(pg1 * p1, axis=1, keepdims=True) * (1.0 / D))
-        ag0 = g0 + dot_wide(pg1s, ua, NT) - beta * (q0 + t)
+        from_later[0].wait_recv()
+        ag0 = got_sg[0] + dot_wide(pg1s, ua, NT) - beta * (q0 + t)
         pg0 = (ag0 * sig0 * (1.0 + pre0 * (1.0 - sig0))).astype(BF).astype(F32)
         gamma = inv0 * inv0 * inv0 * (jnp.sum(pg0 * p0, axis=1, keepdims=True) * (1.0 / D))
         lr[3, my_rows] = (pg0 * inv0).astype(BF)
@@ -524,7 +529,7 @@
             vm((2, ROWS, RANK), F32), vm((2, ROWS, RANK), F32),
             vm((4, 2 * ROWS, RANK), BF), vm((2, 2 * ROWS, 128), F32), vm((2, RANK, 2 * ROWS), BF),
             dma, dma, dma, dma, dma((16, 2)), dma((3,)), dma((3,)),
-            dma((2, 5, 4)), dma((2, 5, 4)), dma((2, 2)), dma((16,)), dma((16,)), dma((5,)), dma((5,)), dma, dma, dma((4,)), dma((4,)),
+            dma((2, 5, 4)), dma((2, 5, 4)), dma((2, 2)), dma((16,)), dma((16,)), dma((5,)), dma((5,)), dma((2,)), dma((2,)), dma((4,)), dma((4,)),
             dma, dma((2, 2, 4)), dma, dma((2, 2, 4)), dma, dma((2, 3)), dma, dma, dma, dma, dma,
         ],
         compiler_params=pltpu.CompilerParams(

time: 134 us -> 130 us (0.970); the launches traced: 134 us -> 128 us
  Pallas kernels: 128 us -> 122 us
    pallas_call x1, Pallas kernels: 128 us -> 122 us  [per_device(): pl.pallas_call(kernel, out_shape=(jax.ShapeDtypeStruct((ROWS, D), BF), ja...]
where the time goes in v4:
time: 130 us; the launch traced here: 128 us
  Pallas kernels  122 us (94%)
  local copies, waits for them, and re-layouts  5.29 us (4%)
    pallas_call x1, Pallas kernels, per_device(): pl.pallas_call(kernel, out_shape=(jax.ShapeDtypeStruct((ROWS, D), BF), ja...  122 us
    unnamed x4, local copies, waits for them, and re-layouts  5.29 us

profile of v4, /device:TPU:2, one launch (start us, length us, event | category | flops | bytes accessed | tf_op | source)
XLA Modules:
  0.0 127.9 jit_solution(10109873367397321176)
XLA Ops:
  0.6 122.0 %relay.1 = (bf16[128,16384]{1,0:T(8,128)(2,1)}, bf16[256,384]{1,0:T(8,128)(2,1)}) custom-call(bf16[128,16384]{1,0:T(8,128)(2,1)} %bitcast.6, bf16[256,384]{1,0:T(8,128)(2,1)} %bitcast.7), custom_call_target="tpu_custom_call" | custom-call | flops 8000000000 | bytes 10000000 | tf_op jit(solution)/shard_map/relay/pallas_call | solution.py:517
  122.6 0.0 copy-start
  122.6 4.6 %copy.6 = bf16[1,2,64,16384]{3,2,1,0:T(8,128)(2,1)} copy(bf16[1,2,64,16384]{3,2,1,0:T(8,128)(2,1)} %bitcast.4) | data formatting | bytes 8388608
  127.2 0.0 copy-done
  127.2 0.7 copy.7
Async XLA Ops:
  122.6 4.6 %copy-start = (bf16[256,384]{1,0:T(8,128)(2,1)S(1)}, bf16[256,384]{1,0:T(8,128)(2,1)}, u32[]{:S(2)}) copy-start(bf16[256,384]{1,0:T(8,128)(2,1)} %get-tuple-element.5) | copy-start | bytes 589828

commit v5 on v4

--- a/solution.py
+++ b/solution.py
@@ -17,7 +17,7 @@
 HALF = D // 2
 BLK = 256
 RING = 4 * BLK
-PACE = ((2, 4, 5, 6, 7, 8, 9), (2, 4, 5, 5, 6, 7, 8, 9))
+PACE = ((4, 8, 10, 12, 14, 16, 18, 18), (4, 8, 10, 10, 12, 14, 16, 18))
 FROM_BACK = (2, 3, 1, 0)
 
 
@@ -111,15 +111,17 @@
     my_rows = pl.ds(pl.multiple_of(c * ROWS, ROWS), ROWS)
     other_rows = pl.ds(pl.multiple_of((1 - c) * ROWS, ROWS), ROWS)
 
-    def exchange(i):
-        for r in range(2):
-            oa, ob = away(i // 4), away(lax.rem(i, 4))
-            for dc in range(2):
-                core = lax.rem(c + dc, 2)
-                a, b = place(r, oa, ob, core)
-                remote(
-                    feed.at[:, feed_at(r, a, b, core)], oth.at[my_rows, block(r, a, b)],
-                    ex_ss, ex_rs.at[i, r], dev(ss=1, dc=dc)).start()
+    def exchange(k):
+        late = k // 24
+        i = (k // 2) * (1 - late) + (12 + lax.rem(k, 4)) * late
+        r = lax.rem(k, 2) * (1 - late) + (7 - k // 4) * late
+        oa, ob = away(i // 4), away(lax.rem(i, 4))
+        for dc in range(2):
+            core = lax.rem(c + dc, 2)
+            a, b = place(r, oa, ob, core)
+            remote(
+                feed.at[:, feed_at(r, a, b, core)], oth.at[my_rows, block(r, a, b)],
+                ex_ss, ex_rs.at[i, r], dev(ss=1, dc=dc)).start()
 
     def fill():
         @pl.loop(0, 32)
@@ -309,13 +311,14 @@
             handed.append(to_core(gram.at[1], got_gram.at[1], 4))
             for copy in handed:
                 copy.wait()
+            pace()
         else:
             for m, k in ((1, 0), (0, 3)):
                 if m == 0:
                     pace()
                     far_products()
                 to_core(part.at[pl.ds(m, 1), other_rows], got_part.at[pl.ds(m, 1)], k).wait()
-                sg[m] = part[m, my_rows] + got_part[m]
+                sg[m] = (part[m, my_rows] + got_part[m]).astype(BF)
                 from_later[m].start()
         return begun, started
 
@@ -327,7 +330,7 @@
     @pl.when(s == 1)
     def _():
         begun, started = gather(1)
-        pl.loop(begun, 16)(exchange)
+        pl.loop(begun, 32)(exchange)
         for copy in from_later:
             copy.wait_send()
         remote(three, three, lr_ss.at[0], lr_rs.at[0], later).wait_recv()
@@ -360,17 +363,17 @@
         sig1 = 1.0 / (1.0 + jnp.exp(-pre1))
         act1 = (pre1 * sig1).astype(BF)
         from_later[1].wait_recv()
-        pg1 = (got_sg[1] * sig1 * (1.0 + pre1 * (1.0 - sig1))).astype(BF).astype(F32)
+        pg1 = (got_sg[1].astype(F32) * sig1 * (1.0 + pre1 * (1.0 - sig1))).astype(BF).astype(F32)
         pg1s = (pg1 * inv1).astype(BF)
         lr[0, my_rows] = act0
         lr[1, my_rows] = pg1s
         lr[2, my_rows] = act1
         to_later = remote(three, three, lr_ss.at[0], lr_rs.at[0], later)
         to_later.start()
-        pl.loop(begun, 16)(exchange)
+        pl.loop(begun, 32)(exchange)
         beta = inv1 * inv1 * inv1 * (jnp.sum(pg1 * p1, axis=1, keepdims=True) * (1.0 / D))
         from_later[0].wait_recv()
-        ag0 = got_sg[0] + dot_wide(pg1s, ua, NT) - beta * (q0 + t)
+        ag0 = got_sg[0].astype(F32) + dot_wide(pg1s, ua, NT) - beta * (q0 + t)
         pg0 = (ag0 * sig0 * (1.0 + pre0 * (1.0 - sig0))).astype(BF).astype(F32)
         gamma = inv0 * inv0 * inv0 * (jnp.sum(pg0 * p0, axis=1, keepdims=True) * (1.0 / D))
         lr[3, my_rows] = (pg0 * inv0).astype(BF)
@@ -392,15 +395,14 @@
 
     top, bottom = pl.ds(0, RANK), pl.ds(RANK, RANK)
 
-    def blocks(n):
+    def blocks(n, both=(1, 0), low=0, high=4):
         oa = FROM_BACK[n]
 
-        @pl.loop(0, 4)
+        @pl.loop(low, high)
         def _(j):
             ob = away(j)
             here = pl.ds(pl.multiple_of(ob * BLK, BLK), BLK)
-            both = range(2)
-            at = [lanes(r, oa, ob) for r in both]
+            at = {r: lanes(r, oa, ob) for r in both}
             for r in both:
                 new = oth.at[:, at[r]]
                 remote(new, new, ex_ss, ex_rs.at[n * 4 + j, r], later).wait_recv()
@@ -411,9 +413,9 @@
 
             def store(done, down, up):
                 if oa == 1:
-                    down = [down[r] + r0[r, 0, :, here].astype(F32) for r in both]
+                    down = {r: down[r] + r0[r, 0, :, here].astype(F32) for r in both}
                 if oa == 3:
-                    up = [up[r] + r0[r, 1, :, here].astype(F32) for r in both]
+                    up = {r: up[r] + r0[r, 1, :, here].astype(F32) for r in both}
                 for r in both:
                     out[:, at[r]] = done[r]
                     gp[top, at[r]] = down[r].astype(BF)
@@ -421,29 +423,29 @@
 
             @pl.when(s == 0)
             def _():
-                x, g = [own[:, at[r]] for r in both], [oth[:, at[r]] for r in both]
-                xf = [x[r].astype(F32) for r in both]
+                x, g = {r: own[:, at[r]] for r in both}, {r: oth[:, at[r]] for r in both}
+                xf = {r: x[r].astype(F32) for r in both}
                 beta = bg[0][:, :1]
                 gamma = bg[1][:, :1]
-                grown = [dot(lr[0], w[pl.ds(0, RANK), at[r]], NN) for r in both]
-                slope = [dot(lr[1], w[pl.ds(2 * RANK, RANK), at[r]], NN) for r in both]
-                bound = [(xf[r] + grown[r]).astype(BF).astype(F32) for r in both]
-                passed = [(g[r].astype(F32) + slope[r] - beta * bound[r]).astype(BF) for r in both]
-                first = [dot(lr[3], w[pl.ds(RANK, RANK), at[r]], NN) for r in both]
-                down = [dot(lrt[0], x[r], NN) for r in both]
-                up = [dot(lrt[1], passed[r], NN) for r in both]
-                done = [(passed[r].astype(F32) + first[r] - gamma * xf[r]).astype(BF) for r in both]
+                grown = {r: dot(lr[0], w[pl.ds(0, RANK), at[r]], NN) for r in both}
+                slope = {r: dot(lr[1], w[pl.ds(2 * RANK, RANK), at[r]], NN) for r in both}
+                bound = {r: (xf[r] + grown[r]).astype(BF).astype(F32) for r in both}
+                passed = {r: (g[r].astype(F32) + slope[r] - beta * bound[r]).astype(BF) for r in both}
+                first = {r: dot(lr[3], w[pl.ds(RANK, RANK), at[r]], NN) for r in both}
+                down = {r: dot(lrt[0], x[r], NN) for r in both}
+                up = {r: dot(lrt[1], passed[r], NN) for r in both}
+                done = {r: (passed[r].astype(F32) + first[r] - gamma * xf[r]).astype(BF) for r in both}
                 store(done, down, up)
 
             @pl.when(s == 1)
             def _():
-                x, g = [oth[:, at[r]] for r in both], [own[:, at[r]] for r in both]
-                grown = [dot(lr[0], w[pl.ds(0, RANK), at[r]], NN) for r in both]
-                final = [dot(lr[2], w[pl.ds(RANK, RANK), at[r]], NN) for r in both]
-                up = [dot(lrt[1], g[r], NN) for r in both]
-                bound = [(x[r].astype(F32) + grown[r]).astype(BF) for r in both]
-                down = [dot(lrt[0], bound[r], NN) for r in both]
-                done = [(bound[r].astype(F32) + final[r]).astype(BF) for r in both]
+                x, g = {r: oth[:, at[r]] for r in both}, {r: own[:, at[r]] for r in both}
+                grown = {r: dot(lr[0], w[pl.ds(0, RANK), at[r]], NN) for r in both}
+                final = {r: dot(lr[2], w[pl.ds(RANK, RANK), at[r]], NN) for r in both}
+                up = {r: dot(lrt[1], g[r], NN) for r in both}
+                bound = {r: (x[r].astype(F32) + grown[r]).astype(BF) for r in both}
+                down = {r: dot(lrt[0], bound[r], NN) for r in both}
+                done = {r: (bound[r].astype(F32) + final[r]).astype(BF) for r in both}
                 store(done, down, up)
 
             for r in both:
@@ -478,9 +480,6 @@
                         remote(
                             gp.at[:, at[r]], r2.at[r, ob - 1], p2_ss, p2_rs.at[r, ob - 1], along(r, ob, True)).start()
 
-    for n in range(4):
-        blocks(n)
-
     def summed(r):
         total = tot[r]
         for k in range(3):
@@ -488,9 +487,14 @@
             total += r2[r, k].astype(F32)
         return total
 
+    for n in range(3):
+        blocks(n)
+    blocks(3, (1,))
+    blocks(3, (0,), 0, 2)
     send3[...] = summed(1).astype(BF)
     across = remote(send3, r3, p3_ss, p3_rs, dev(dx=1))
     across.start()
+    blocks(3, (0,), 2, 4)
     total = summed(0)
     across.wait()
     wg[...] = (total + r3[...].astype(F32)).T.astype(BF)
@@ -526,7 +530,7 @@
             vm((2, 2 * RANK, BLK), F32), vm((2 * RANK, BLK), BF), vm((2 * RANK, BLK), BF),
             vm((3, 2 * ROWS, RANK), F32), vm((2, RANK, RANK), F32), vm((2 * ROWS, 128), F32),
             vm((3, ROWS, RANK), F32), vm((2, RANK, RANK), F32), vm((ROWS, 128), F32),
-            vm((2, ROWS, RANK), F32), vm((2, ROWS, RANK), F32),
+            vm((2, ROWS, RANK), BF), vm((2, ROWS, RANK), BF),
             vm((4, 2 * ROWS, RANK), BF), vm((2, 2 * ROWS, 128), F32), vm((2, RANK, 2 * ROWS), BF),
             dma, dma, dma, dma, dma((16, 2)), dma((3,)), dma((3,)),
             dma((2, 5, 4)), dma((2, 5, 4)), dma((2, 2)), dma((16,)), dma((16,)), dma((5,)), dma((5,)), dma((2,)), dma((2,)), dma((4,)), dma((4,)),

time: 130 us -> 126 us (0.969); the launches traced: 128 us -> 126 us
  Pallas kernels: 122 us -> 120 us
    pallas_call x1, Pallas kernels: 122 us -> 120 us  [per_device(): pl.pallas_call(kernel, out_shape=(jax.ShapeDtypeStruct((ROWS, D), BF), ja...]
where the time goes in v5:
time: 126 us
  Pallas kernels  120 us (95%)
  local copies, waits for them, and re-layouts  5.29 us (4%)
    pallas_call x1, Pallas kernels, per_device(): pl.pallas_call(kernel, out_shape=(jax.ShapeDtypeStruct((ROWS, D), BF), ja...  120 us
    unnamed x4, local copies, waits for them, and re-layouts  5.29 us

profile of v5, /device:TPU:2, one launch (start us, length us, event | category | flops | bytes accessed | tf_op | source)
XLA Modules:
  0.0 126.2 jit_solution(11084413475673507447)
XLA Ops:
  0.6 120.3 %relay.1 = (bf16[128,16384]{1,0:T(8,128)(2,1)}, bf16[256,384]{1,0:T(8,128)(2,1)}) custom-call(bf16[128,16384]{1,0:T(8,128)(2,1)} %bitcast.6, bf16[256,384]{1,0:T(8,128)(2,1)} %bitcast.7), custom_call_target="tpu_custom_call" | custom-call | flops 8000000000 | bytes 10000000 | tf_op jit(solution)/shard_map/relay/pallas_call | solution.py:521
  120.9 0.0 copy-start
  120.9 4.6 %copy.6 = bf16[1,2,64,16384]{3,2,1,0:T(8,128)(2,1)} copy(bf16[1,2,64,16384]{3,2,1,0:T(8,128)(2,1)} %bitcast.4) | data formatting | bytes 8388608
  125.6 0.0 copy-done
  125.6 0.7 copy.7
Async XLA Ops:
  120.9 4.6 %copy-start = (bf16[256,384]{1,0:T(8,128)(2,1)S(1)}, bf16[256,384]{1,0:T(8,128)(2,1)}, u32[]{:S(2)}) copy-start(bf16[256,384]{1,0:T(8,128)(2,1)} %get-tuple-element.5) | copy-start | bytes 589828

commit v6 on v5

--- a/solution.py
+++ b/solution.py
@@ -537,7 +537,7 @@
             dma, dma((2, 2, 4)), dma, dma((2, 2, 4)), dma, dma((2, 3)), dma, dma, dma, dma, dma,
         ],
         compiler_params=pltpu.CompilerParams(
-            collective_id=0, has_side_effects=True, vmem_limit_bytes=60 * 2**20),
+            collective_id=0, has_side_effects=True, vmem_limit_bytes=44 * 2**20),
         cost_estimate=pl.CostEstimate(flops=8 * 10**9, bytes_accessed=10**7, transcendentals=0),
         name="relay",
     )(feed, shard)

time: 126 us -> 125 us (level)
  Pallas kernels: 120 us -> 118 us
    pallas_call x1, Pallas kernels: 120 us -> 118 us  [per_device(): pl.pallas_call(kernel, out_shape=(jax.ShapeDtypeStruct((ROWS, D), BF), ja...]
    unnamed x4 -> x6, local copies, waits for them, and re-layouts: 5.29 us -> 5.8 us
where the time goes in v6:
time: 125 us
  Pallas kernels  118 us (94%)
  local copies, waits for them, and re-layouts  5.8 us (5%)
    pallas_call x1, Pallas kernels, per_device(): pl.pallas_call(kernel, out_shape=(jax.ShapeDtypeStruct((ROWS, D), BF), ja...  118 us
    unnamed x6, local copies, waits for them, and re-layouts  5.8 us

profile of v6, /device:TPU:2, one launch (start us, length us, event | category | flops | bytes accessed | tf_op | source)
XLA Modules:
  0.0 124.9 jit_solution(18414982325654260482)
XLA Ops:
  0.6 0.0 copy-start
  0.6 2.2 %copy-done = bf16[1,2,64,16384]{3,2,1,0:T(8,128)(2,1)S(1)} copy-done((bf16[1,2,64,16384]{3,2,1,0:T(8,128)(2,1)S(1)}, bf16[1,2,64,16384]{3,2,1,0:T(8,128)(2,1)}, u32[]{:S(2)}) %copy-start) | copy-done | bytes 4194328
  2.8 0.0 copy-start.1
  2.8 0.9 copy-done.1
  3.7 118.5 %relay.1 = (bf16[128,16384]{1,0:T(8,128)(2,1)S(1)}, bf16[256,384]{1,0:T(8,128)(2,1)S(1)}) custom-call(bf16[128,16384]{1,0:T(8,128)(2,1)S(1)} %bitcast.6, bf16[256,384]{1,0:T(8,128)(2,1)S(1)} %bitcast.7), custom_call_target="tpu_custom_call" | custom-call | flops 8000000000 | bytes 10000000 | tf_op jit(solution)/shard_map/relay/pallas_call | solution.py:521
  122.2 2.0 %copy.6 = bf16[1,2,64,16384]{3,2,1,0:T(8,128)(2,1)} copy(bf16[1,2,64,16384]{3,2,1,0:T(8,128)(2,1)S(1)} %bitcast.4) | data formatting | bytes 8388608
  124.2 0.7 copy.7
Async XLA Ops:
  0.6 2.2 %copy-start = (bf16[1,2,64,16384]{3,2,1,0:T(8,128)(2,1)S(1)}, bf16[1,2,64,16384]{3,2,1,0:T(8,128)(2,1)}, u32[]{:S(2)}) copy-start(bf16[1,2,64,16384]{3,2,1,0:T(8,128)(2,1)} %param.2) | copy-start | bytes 12582916
  2.8 0.9 copy-start.1
